TPU v7x, 512 devices: a whole 4x8x8 slice. The times are simulated.
512 devices in a mesh: wide: 128 (over z_lo, y, x), narrow: 4 (over z_hi, core).
Axes of the slice: x: 4, y: 8, z: 8 (z_hi: 2, z_lo: 4; z = z_hi * 4 + z_lo), core: 2. Of those that a mesh axis runs over, the one named last changes fastest.
Arguments:
- adjoint_velocity: float32 [3, 2048, 128, 128], P(None, 'wide', 'narrow'), may hold values from -60 to 60
- coefficient: float32 [2048, 128, 128], P('wide', 'narrow'), may hold values from 0.5 to 2
- record_counts: int32 [128, 4], P('wide', 'narrow'), may hold values from 256 to 1024, as said below
- record_cells: int32 [128, 4, 3, 1024], P('wide', 'narrow'), may hold values from 0 to 127, as said below
- record_offsets: float32 [128, 4, 3, 1024], P('wide', 'narrow'), may hold values from 0 to 1
Outputs:
- smoothed: float32 [3, 2048, 128, 128], P(None, 'wide', 'narrow')
- moment_grad: float32 [128, 4, 12, 1024], P('wide', 'narrow')
Inputs may be any that keep to these rules, and one draw needn't show every extreme that they name: Slots 0 to record_counts - 1 of a tile hold live records, the others padding; in every draw some tile has all 1024 slots live. `record_cells`: component 0 lies in 0 to 15, component 1 in 0 to 31, component 2 in 0 to 127. Of a tile's 1024 slots, exactly 256 have component 0 below 4 and exactly 256 have it at 12 or above; exactly 128 have component 1 below 4 and exactly 128 have it at 28 or above; each of the four pairings of a low or high component 0 with a low or high component 1 holds exactly 32 slots.
All inputs are finite; a program needn't handle non-finite values.
Results may differ from a plain program's by a relative error of at most 0.0003.
Values sent between devices are 32-bit elements; how exact they have to be, the bound alone decides.
A program may use at most 64 MiB of HBM per device.

v0:
```python
import math

import jax
import jax.numpy as jnp
from jax import lax
from jax.sharding import PartitionSpec as P

RADIUS = 4
SWEEPS = 4


envelope_width = 1.25
relax_factor = 0.8
diag_shift = 1.0


def extended_2(block, sides, width):
    for axis, dim in sides:
        count = lax.axis_size(axis)
        forward = [(i, i + 1) for i in range(count - 1)]
        backward = [(target, source) for source, target in forward]
        low = lax.ppermute(
            lax.slice_in_dim(block, block.shape[dim] - width, None, axis=dim), axis, forward
        )
        high = lax.ppermute(lax.slice_in_dim(block, 0, width, axis=dim), axis, backward)
        block = jnp.concatenate([low, block, high], axis=dim)
    return block


def profile(distance):
    width_sq = envelope_width * envelope_width
    base = jnp.exp(-distance * distance / (2.0 * width_sq)) / (
        envelope_width * math.sqrt(2.0 * math.pi)
    )
    first = -distance / width_sq * base
    second = (distance * distance / width_sq - 1.0) / width_sq * base
    return (base, first, second)


def neighbour_views(padded):
    return [
        padded[..., 2:, 1:-1, 1:-1],
        padded[..., :-2, 1:-1, 1:-1],
        padded[..., 1:-1, 2:, 1:-1],
        padded[..., 1:-1, :-2, 1:-1],
        padded[..., 1:-1, 1:-1, 2:],
        padded[..., 1:-1, 1:-1, :-2],
    ]


def axis_weights(length, centre, offset):
    places = jnp.arange(length, dtype=jnp.float32)[:, None]
    inside = jnp.abs(places - centre[None, :]) <= RADIUS
    weights = profile(places + 0.5 - centre[None, :] - offset[None, :])
    return [jnp.where(inside, item, jnp.zeros_like(item)) for item in weights]


def block_moments(field, centres, offsets, alive):
    highest = lax.Precision.HIGHEST
    length_x, length_y, length_z = (field.shape[1], field.shape[2], field.shape[3])
    flat = field.reshape(3 * length_x * length_y, length_z)
    slots = centres.shape[1]
    padded_slots = (slots + 127) // 128 * 128
    blocks = padded_slots // 128

    def one_block(inputs):
        centre, offset, live = inputs
        wx0, wx1, wx2 = [
            item * live[None, :] for item in axis_weights(length_x, centre[0], offset[0])
        ]
        wy0, wy1, wy2 = axis_weights(length_y, centre[1], offset[1])
        wz = jnp.concatenate(axis_weights(length_z, centre[2], offset[2]), axis=1)
        zed = jnp.dot(flat, wz, precision=highest).reshape(3, length_x, length_y, 3, 128)
        along = jnp.einsum("ixykp,yp->ixkp", zed, wy0, precision=highest)
        slope = jnp.einsum("ixyp,yp->ixp", zed[:, :, :, 0], wy1, precision=highest)
        bend = jnp.einsum("ixyp,yp->ixp", zed[:, :, :, 0], wy2, precision=highest)
        dip_x = jnp.einsum("ixp,xp->ip", along[:, :, 0], wx1, precision=highest)
        dip_y = jnp.einsum("ixp,xp->ip", slope, wx0, precision=highest)
        dip_z = jnp.einsum("ixp,xp->ip", along[:, :, 1], wx0, precision=highest)
        quad = jnp.einsum("ixp,xp->ip", along[:, :, 0], wx2, precision=highest) + jnp.einsum(
            "ixp,xp->ip", bend + along[:, :, 2], wx0, precision=highest
        )
        return jnp.stack([dip_x, dip_y, dip_z, quad], axis=1).reshape(12, 128)

    centre_blocks = centres.reshape(3, blocks, 128).transpose(1, 0, 2)
    offset_blocks = offsets.reshape(3, blocks, 128).transpose(1, 0, 2)
    alive_blocks = alive.reshape(blocks, 128)
    result = lax.map(one_block, (centre_blocks, offset_blocks, alive_blocks))
    return result.transpose(1, 0, 2).reshape(12, padded_slots)


def body(adjoint_velocity, coefficient, record_counts, record_cells, record_offsets):
    coef_padded = extended_2(coefficient, (("wide", 0), ("narrow", 1)), 1)
    coef_padded = jnp.pad(coef_padded, ((0, 0), (0, 0), (1, 1)))
    faces = [0.5 * (coefficient + view) for view in neighbour_views(coef_padded)]
    total = diag_shift + sum(faces)
    smoothed = relax_factor * adjoint_velocity / total
    for sweep in range(SWEEPS - 1):
        padded = extended_2(smoothed, (("wide", 1), ("narrow", 2)), 1)
        padded = jnp.pad(padded, ((0, 0), (0, 0), (0, 0), (1, 1)))
        beside_all = sum((face * view for face, view in zip(faces, neighbour_views(padded))))
        smoothed = (
            smoothed + relax_factor * (adjoint_velocity - total * smoothed + beside_all) / total
        )
    slots = record_cells.shape[3]
    cells_int = record_cells[0, 0]
    centres = cells_int.astype(jnp.float32)
    offsets = record_offsets[0, 0]
    alive = (jnp.arange(slots, dtype=jnp.int32) < record_counts[0, 0]).astype(jnp.float32)
    extended = extended_2(smoothed, (("wide", 1), ("narrow", 2)), RADIUS)
    lifted = centres + jnp.array([RADIUS, RADIUS, 0], jnp.float32)[:, None]
    grads = block_moments(extended, lifted, offsets, alive)
    return (smoothed, grads[None, None])


def solution(mesh):
    return jax.shard_map(
        body,
        mesh=mesh,
        in_specs=(
            P(None, "wide", "narrow", None),
            P("wide", "narrow", None),
            P("wide", "narrow"),
            P("wide", "narrow", None, None),
            P("wide", "narrow", None, None),
        ),
        out_specs=(P(None, "wide", "narrow", None), P("wide", "narrow", None, None)),
        check_vma=False,
    )
```

profile of v0, /device:TPU:63, one launch (start us, length us, event | category | flops | bytes accessed | tf_op | source)
XLA Modules:
  0.0 309.8 jit_solution(11760605361437879754)
XLA Ops:
  1.4 3.1 %collective-permute-start.1 = (f32[1,32,128]{2,1,0:T(8,128)S(1)}, f32[1,32,128]{2,1,0:T(8,128)S(1)}, u32[]{:S(2)}, u32[]{:S(2)}) collective-permute-start(f32[1,32,128]{2,1,0:T(8,128)S(1)} %get-tuple-element.169), channel_id=1, source_target_pairs={{0,4},{4,8},{8,12},{12,16},{16,20},{20,24},{24,28},{28,32},{32,36}... | collective-permute-start | bytes 49160 | tf_op jit(solution)/shard_map/ppermute | solution.py:22
  4.5 2.2 collective-permute-start
  7.7 5.5 %collective-permute-done = f32[1,32,128]{2,1,0:T(8,128)S(1)} collective-permute-done((f32[1,32,128]{2,1,0:T(8,128)S(1)}, f32[1,32,128]{2,1,0:T(8,128)S(1)}, u32[]{:S(2)}, u32[]{:S(2)}) %collective-permute-start) | collective-permute-done | bytes 16416 | tf_op jit(solution)/shard_map/ppermute | solution.py:25
  13.2 4.0 %collective-permute-start.2 = (f32[18,1,128]{2,1,0:T(1,128)S(1)}, f32[18,1,128]{2,1,0:T(1,128)S(1)}, u32[]{:S(2)}, u32[]{:S(2)}) collective-permute-start(f32[18,1,128]{2,1,0:T(1,128)S(1)} %get-tuple-element.167), channel_id=1, source_target_pairs={{1,0},{2,1},{3,2},{5,4},{6,5},{7,6},{9,8},{10,9},{11,10},{13,12},{... | collective-permute-start | bytes 27656 | tf_op jit(solution)/shard_map/ppermute | solution.py:25
  17.2 9.6 %collective-permute-start.3 = (f32[18,1,128]{2,1,0:T(1,128)S(1)}, f32[18,1,128]{2,1,0:T(1,128)S(1)}, u32[]{:S(2)}, u32[]{:S(2)}) collective-permute-start(f32[18,1,128]{2,1,0:T(1,128)S(1)} %get-tuple-element.166), channel_id=1, source_target_pairs={{0,1},{1,2},{2,3},{4,5},{5,6},{6,7},{8,9},{9,10},{10,11},{12,13},{... | collective-permute-start | bytes 27656 | tf_op jit(solution)/shard_map/ppermute | solution.py:22
  29.7 1.9 collective-permute-start.4
  31.6 7.6 %collective-permute-start.5 = (f32[3,1,32,128]{3,2,1,0:T(8,128)S(1)}, f32[3,1,32,128]{3,2,1,0:T(8,128)S(1)}, u32[]{:S(2)}, u32[]{:S(2)}) collective-permute-start(f32[3,1,32,128]{3,2,1,0:T(8,128)S(1)} %get-tuple-element.164), channel_id=1, source_target_pairs={{0,4},{4,8},{8,12},{12,16},{16,20},{20,24},{24,28},{28,32},{32,36}... | collective-permute-start | bytes 147464 | tf_op jit(solution)/shard_map/ppermute | solution.py:22
  40.4 1.9 collective-permute-start.6
  42.4 9.2 %collective-permute-start.7 = (f32[3,18,1,128]{3,2,1,0:T(1,128)S(1)}, f32[3,18,1,128]{3,2,1,0:T(1,128)S(1)}, u32[]{:S(2)}, u32[]{:S(2)}) collective-permute-start(f32[3,18,1,128]{3,2,1,0:T(1,128)S(1)} %get-tuple-element.156), channel_id=1, source_target_pairs={{0,1},{1,2},{2,3},{4,5},{5,6},{6,7},{8,9},{9,10},{10,11},{12,13},{... | collective-permute-start | bytes 82952 | tf_op jit(solution)/shard_map/ppermute | solution.py:22
  54.3 1.9 collective-permute-start.8
  56.2 8.2 %collective-permute-start.9 = (f32[3,1,32,128]{3,2,1,0:T(8,128)S(1)}, f32[3,1,32,128]{3,2,1,0:T(8,128)S(1)}, u32[]{:S(2)}, u32[]{:S(2)}) collective-permute-start(f32[3,1,32,128]{3,2,1,0:T(8,128)S(1)} %get-tuple-element.162), channel_id=1, source_target_pairs={{0,4},{4,8},{8,12},{12,16},{16,20},{20,24},{24,28},{28,32},{32,36}... | collective-permute-start | bytes 147464 | tf_op jit(solution)/shard_map/ppermute | solution.py:22
  65.6 1.9 collective-permute-start.10
  67.5 9.0 %collective-permute-start.11 = (f32[3,18,1,128]{3,2,1,0:T(1,128)S(1)}, f32[3,18,1,128]{3,2,1,0:T(1,128)S(1)}, u32[]{:S(2)}, u32[]{:S(2)}) collective-permute-start(f32[3,18,1,128]{3,2,1,0:T(1,128)S(1)} %get-tuple-element.154), channel_id=1, source_target_pairs={{0,1},{1,2},{2,3},{4,5},{5,6},{6,7},{8,9},{9,10},{10,11},{12,13},{... | collective-permute-start | bytes 82952 | tf_op jit(solution)/shard_map/ppermute | solution.py:22
  79.2 1.9 collective-permute-start.12
  81.1 8.2 %collective-permute-start.13 = (f32[3,1,32,128]{3,2,1,0:T(8,128)S(1)}, f32[3,1,32,128]{3,2,1,0:T(8,128)S(1)}, u32[]{:S(2)}, u32[]{:S(2)}) collective-permute-start(f32[3,1,32,128]{3,2,1,0:T(8,128)S(1)} %get-tuple-element.160), channel_id=1, source_target_pairs={{0,4},{4,8},{8,12},{12,16},{16,20},{20,24},{24,28},{28,32},{32,36}... | collective-permute-start | bytes 147464 | tf_op jit(solution)/shard_map/ppermute | solution.py:22
  90.5 1.9 collective-permute-start.14
  92.5 9.0 %collective-permute-start.15 = (f32[3,18,1,128]{3,2,1,0:T(1,128)S(1)}, f32[3,18,1,128]{3,2,1,0:T(1,128)S(1)}, u32[]{:S(2)}, u32[]{:S(2)}) collective-permute-start(f32[3,18,1,128]{3,2,1,0:T(1,128)S(1)} %get-tuple-element.152), channel_id=1, source_target_pairs={{0,1},{1,2},{2,3},{4,5},{5,6},{6,7},{8,9},{9,10},{10,11},{12,13},{... | collective-permute-start | bytes 82952 | tf_op jit(solution)/shard_map/ppermute | solution.py:22
  104.2 8.2 %collective-permute-start.16 = (f32[3,4,32,128]{3,2,1,0:T(8,128)S(1)}, f32[3,4,32,128]{3,2,1,0:T(8,128)S(1)}, u32[]{:S(2)}, u32[]{:S(2)}) collective-permute-start(f32[3,4,32,128]{3,2,1,0:T(8,128)S(1)} %get-tuple-element.158), channel_id=1, source_target_pairs={{0,4},{4,8},{8,12},{12,16},{16,20},{20,24},{24,28},{28,32},{32,36}... | collective-permute-start | bytes 589832 | tf_op jit(solution)/shard_map/ppermute | solution.py:22
  112.4 1.9 collective-permute-start.17
  115.0 8.3 %collective-permute-done.17 = f32[3,4,32,128]{3,2,1,0:T(8,128)S(1)} collective-permute-done((f32[3,4,32,128]{3,2,1,0:T(8,128)S(1)}, f32[3,4,32,128]{3,2,1,0:T(8,128)S(1)}, u32[]{:S(2)}, u32[]{:S(2)}) %collective-permute-start.17) | collective-permute-done | bytes 196640 | tf_op jit(solution)/shard_map/ppermute | solution.py:25
  123.3 9.4 %collective-permute-start.18 = (f32[3,24,4,128]{3,2,1,0:T(4,128)S(1)}, f32[3,24,4,128]{3,2,1,0:T(4,128)S(1)}, u32[]{:S(2)}, u32[]{:S(2)}) collective-permute-start(f32[3,24,4,128]{3,2,1,0:T(4,128)S(1)} %get-tuple-element.150), channel_id=1, source_target_pairs={{0,1},{1,2},{2,3},{4,5},{5,6},{6,7},{8,9},{9,10},{10,11},{12,13},{... | collective-permute-start | bytes 442376 | tf_op jit(solution)/shard_map/ppermute | solution.py:22
  132.7 2.1 collective-permute-start.19
  135.6 8.0 %collective-permute-done.19 = f32[3,24,4,128]{3,2,1,0:T(4,128)S(1)} collective-permute-done((f32[3,24,4,128]{3,2,1,0:T(4,128)S(1)}, f32[3,24,4,128]{3,2,1,0:T(4,128)S(1)}, u32[]{:S(2)}, u32[]{:S(2)}) %collective-permute-start.19) | collective-permute-done | bytes 147488 | tf_op jit(solution)/shard_map/ppermute | solution.py:25
  143.9 165.3 %while.13 = (s32[]{:T(128)}, f32[8,12,128]{2,1,0:T(8,128)S(1)}, f32[8,3,128]{2,0,1:T(8,128)S(1)}, f32[8,3,128]{2,0,1:T(8,128)}, f32[8,128]{1,0:T(8,128)S(1)}, /*...) while((s32[]{:T(128)}, f32[8,12,128]{2,1,0:T(8,128)S(1)}, f32[8,3,128]{2,0,1:T(8,128)S(1)}, ...), condition=%wide.region_1.2_spmd, body=%wide.region_0.1_spmd.sunk | while | flops 1703012480 | bytes 26438824 | solution.py:88
  144.7 5.2 %convolution_bitcast_fusion.2 = f32[2880,384]{1,0:T(8,128)} fusion(f32[2880,128]{1,0:T(8,128)S(1)} %get-tuple-element.274, f32[128,128]{1,0:T(8,128)S(1)} %get-tuple-element.230, f32[128,128]{1,0:T(8,128)S(1)} %get-tuple-element.231, f32[128,128]{1,0:T(8,128)S(1)} %get-tuple-element.232), kind=kOutput, calls=%fused_computation.1.clone.1 | convolution fusion | flops 1698791424 | bytes 6094848 | tf_op jit(solution)/shard_map/while/body/eval_jaxpr/dot_general | solution.py:73
  149.9 7.5 %reshape.79 = f32[3,24,40,3,128]{4,3,2,1,0:T(4,128)} reshape(f32[2880,384]{1,0:T(8,128)} %convolution_bitcast_fusion.2) | data formatting | bytes 8847360 | tf_op jit(solution)/shard_map/while/body/eval_jaxpr/reshape | solution.py:73
  160.0 4.4 %multiply_reduce_fusion.8 = f32[128,3,24,3]{0,3,2,1:T(4,128)S(1)} fusion(f32[3,24,40,3,128]{4,3,2,1,0:T(4,128)} %reshape.79, f32[128,40]{0,1:T(8,128)S(1)} %get-tuple-element.235), kind=kLoop, calls=%fused_computation.clone.1 | loop fusion | flops 2184192 | bytes 4554752 | tf_op jit(solution)/shard_map/while
  165.4 5.2 %convolution_bitcast_fusion.2 = f32[2880,384]{1,0:T(8,128)} fusion(f32[2880,128]{1,0:T(8,128)S(1)} %get-tuple-element.274, f32[128,128]{1,0:T(8,128)S(1)} %get-tuple-element.230, f32[128,128]{1,0:T(8,128)S(1)} %get-tuple-element.231, f32[128,128]{1,0:T(8,128)S(1)} %get-tuple-element.232), kind=kOutput, calls=%fused_computation.1.clone.1 | convolution fusion | flops 1698791424 | bytes 6094848 | tf_op jit(solution)/shard_map/while/body/eval_jaxpr/dot_general | solution.py:73
  170.6 7.5 %reshape.79 = f32[3,24,40,3,128]{4,3,2,1,0:T(4,128)} reshape(f32[2880,384]{1,0:T(8,128)} %convolution_bitcast_fusion.2) | data formatting | bytes 8847360 | tf_op jit(solution)/shard_map/while/body/eval_jaxpr/reshape | solution.py:73
  180.6 4.4 %multiply_reduce_fusion.8 = f32[128,3,24,3]{0,3,2,1:T(4,128)S(1)} fusion(f32[3,24,40,3,128]{4,3,2,1,0:T(4,128)} %reshape.79, f32[128,40]{0,1:T(8,128)S(1)} %get-tuple-element.235), kind=kLoop, calls=%fused_computation.clone.1 | loop fusion | flops 2184192 | bytes 4554752 | tf_op jit(solution)/shard_map/while
  186.1 5.2 %convolution_bitcast_fusion.2 = f32[2880,384]{1,0:T(8,128)} fusion(f32[2880,128]{1,0:T(8,128)S(1)} %get-tuple-element.274, f32[128,128]{1,0:T(8,128)S(1)} %get-tuple-element.230, f32[128,128]{1,0:T(8,128)S(1)} %get-tuple-element.231, f32[128,128]{1,0:T(8,128)S(1)} %get-tuple-element.232), kind=kOutput, calls=%fused_computation.1.clone.1 | convolution fusion | flops 1698791424 | bytes 6094848 | tf_op jit(solution)/shard_map/while/body/eval_jaxpr/dot_general | solution.py:73
  191.2 7.5 %reshape.79 = f32[3,24,40,3,128]{4,3,2,1,0:T(4,128)} reshape(f32[2880,384]{1,0:T(8,128)} %convolution_bitcast_fusion.2) | data formatting | bytes 8847360 | tf_op jit(solution)/shard_map/while/body/eval_jaxpr/reshape | solution.py:73
  201.3 4.4 %multiply_reduce_fusion.8 = f32[128,3,24,3]{0,3,2,1:T(4,128)S(1)} fusion(f32[3,24,40,3,128]{4,3,2,1,0:T(4,128)} %reshape.79, f32[128,40]{0,1:T(8,128)S(1)} %get-tuple-element.235), kind=kLoop, calls=%fused_computation.clone.1 | loop fusion | flops 2184192 | bytes 4554752 | tf_op jit(solution)/shard_map/while
  206.7 5.2 %convolution_bitcast_fusion.2 = f32[2880,384]{1,0:T(8,128)} fusion(f32[2880,128]{1,0:T(8,128)S(1)} %get-tuple-element.274, f32[128,128]{1,0:T(8,128)S(1)} %get-tuple-element.230, f32[128,128]{1,0:T(8,128)S(1)} %get-tuple-element.231, f32[128,128]{1,0:T(8,128)S(1)} %get-tuple-element.232), kind=kOutput, calls=%fused_computation.1.clone.1 | convolution fusion | flops 1698791424 | bytes 6094848 | tf_op jit(solution)/shard_map/while/body/eval_jaxpr/dot_general | solution.py:73
  211.9 7.5 %reshape.79 = f32[3,24,40,3,128]{4,3,2,1,0:T(4,128)} reshape(f32[2880,384]{1,0:T(8,128)} %convolution_bitcast_fusion.2) | data formatting | bytes 8847360 | tf_op jit(solution)/shard_map/while/body/eval_jaxpr/reshape | solution.py:73
  222.0 4.4 %multiply_reduce_fusion.8 = f32[128,3,24,3]{0,3,2,1:T(4,128)S(1)} fusion(f32[3,24,40,3,128]{4,3,2,1,0:T(4,128)} %reshape.79, f32[128,40]{0,1:T(8,128)S(1)} %get-tuple-element.235), kind=kLoop, calls=%fused_computation.clone.1 | loop fusion | flops 2184192 | bytes 4554752 | tf_op jit(solution)/shard_map/while
  227.4 5.2 %convolution_bitcast_fusion.2 = f32[2880,384]{1,0:T(8,128)} fusion(f32[2880,128]{1,0:T(8,128)S(1)} %get-tuple-element.274, f32[128,128]{1,0:T(8,128)S(1)} %get-tuple-element.230, f32[128,128]{1,0:T(8,128)S(1)} %get-tuple-element.231, f32[128,128]{1,0:T(8,128)S(1)} %get-tuple-element.232), kind=kOutput, calls=%fused_computation.1.clone.1 | convolution fusion | flops 1698791424 | bytes 6094848 | tf_op jit(solution)/shard_map/while/body/eval_jaxpr/dot_general | solution.py:73
  232.6 7.5 %reshape.79 = f32[3,24,40,3,128]{4,3,2,1,0:T(4,128)} reshape(f32[2880,384]{1,0:T(8,128)} %convolution_bitcast_fusion.2) | data formatting | bytes 8847360 | tf_op jit(solution)/shard_map/while/body/eval_jaxpr/reshape | solution.py:73
  242.6 4.4 %multiply_reduce_fusion.8 = f32[128,3,24,3]{0,3,2,1:T(4,128)S(1)} fusion(f32[3,24,40,3,128]{4,3,2,1,0:T(4,128)} %reshape.79, f32[128,40]{0,1:T(8,128)S(1)} %get-tuple-element.235), kind=kLoop, calls=%fused_computation.clone.1 | loop fusion | flops 2184192 | bytes 4554752 | tf_op jit(solution)/shard_map/while
  248.1 5.2 %convolution_bitcast_fusion.2 = f32[2880,384]{1,0:T(8,128)} fusion(f32[2880,128]{1,0:T(8,128)S(1)} %get-tuple-element.274, f32[128,128]{1,0:T(8,128)S(1)} %get-tuple-element.230, f32[128,128]{1,0:T(8,128)S(1)} %get-tuple-element.231, f32[128,128]{1,0:T(8,128)S(1)} %get-tuple-element.232), kind=kOutput, calls=%fused_computation.1.clone.1 | convolution fusion | flops 1698791424 | bytes 6094848 | tf_op jit(solution)/shard_map/while/body/eval_jaxpr/dot_general | solution.py:73
  253.2 7.5 %reshape.79 = f32[3,24,40,3,128]{4,3,2,1,0:T(4,128)} reshape(f32[2880,384]{1,0:T(8,128)} %convolution_bitcast_fusion.2) | data formatting | bytes 8847360 | tf_op jit(solution)/shard_map/while/body/eval_jaxpr/reshape | solution.py:73
  263.3 4.4 %multiply_reduce_fusion.8 = f32[128,3,24,3]{0,3,2,1:T(4,128)S(1)} fusion(f32[3,24,40,3,128]{4,3,2,1,0:T(4,128)} %reshape.79, f32[128,40]{0,1:T(8,128)S(1)} %get-tuple-element.235), kind=kLoop, calls=%fused_computation.clone.1 | loop fusion | flops 2184192 | bytes 4554752 | tf_op jit(solution)/shard_map/while
  268.7 5.2 %convolution_bitcast_fusion.2 = f32[2880,384]{1,0:T(8,128)} fusion(f32[2880,128]{1,0:T(8,128)S(1)} %get-tuple-element.274, f32[128,128]{1,0:T(8,128)S(1)} %get-tuple-element.230, f32[128,128]{1,0:T(8,128)S(1)} %get-tuple-element.231, f32[128,128]{1,0:T(8,128)S(1)} %get-tuple-element.232), kind=kOutput, calls=%fused_computation.1.clone.1 | convolution fusion | flops 1698791424 | bytes 6094848 | tf_op jit(solution)/shard_map/while/body/eval_jaxpr/dot_general | solution.py:73
  273.9 7.5 %reshape.79 = f32[3,24,40,3,128]{4,3,2,1,0:T(4,128)} reshape(f32[2880,384]{1,0:T(8,128)} %convolution_bitcast_fusion.2) | data formatting | bytes 8847360 | tf_op jit(solution)/shard_map/while/body/eval_jaxpr/reshape | solution.py:73
  284.0 4.4 %multiply_reduce_fusion.8 = f32[128,3,24,3]{0,3,2,1:T(4,128)S(1)} fusion(f32[3,24,40,3,128]{4,3,2,1,0:T(4,128)} %reshape.79, f32[128,40]{0,1:T(8,128)S(1)} %get-tuple-element.235), kind=kLoop, calls=%fused_computation.clone.1 | loop fusion | flops 2184192 | bytes 4554752 | tf_op jit(solution)/shard_map/while
  289.4 5.2 %convolution_bitcast_fusion.2 = f32[2880,384]{1,0:T(8,128)} fusion(f32[2880,128]{1,0:T(8,128)S(1)} %get-tuple-element.274, f32[128,128]{1,0:T(8,128)S(1)} %get-tuple-element.230, f32[128,128]{1,0:T(8,128)S(1)} %get-tuple-element.231, f32[128,128]{1,0:T(8,128)S(1)} %get-tuple-element.232), kind=kOutput, calls=%fused_computation.1.clone.1 | convolution fusion | flops 1698791424 | bytes 6094848 | tf_op jit(solution)/shard_map/while/body/eval_jaxpr/dot_general | solution.py:73
  294.6 7.5 %reshape.79 = f32[3,24,40,3,128]{4,3,2,1,0:T(4,128)} reshape(f32[2880,384]{1,0:T(8,128)} %convolution_bitcast_fusion.2) | data formatting | bytes 8847360 | tf_op jit(solution)/shard_map/while/body/eval_jaxpr/reshape | solution.py:73
  304.6 4.4 %multiply_reduce_fusion.8 = f32[128,3,24,3]{0,3,2,1:T(4,128)S(1)} fusion(f32[3,24,40,3,128]{4,3,2,1,0:T(4,128)} %reshape.79, f32[128,40]{0,1:T(8,128)S(1)} %get-tuple-element.235), kind=kLoop, calls=%fused_computation.clone.1 | loop fusion | flops 2184192 | bytes 4554752 | tf_op jit(solution)/shard_map/while
  (253 shorter events, 45.5 us)
Async XLA Ops:
  1.4 5.3 %collective-permute-start.1 = (f32[1,32,128]{2,1,0:T(8,128)S(1)}, f32[1,32,128]{2,1,0:T(8,128)S(1)}, u32[]{:S(2)}, u32[]{:S(2)}) collective-permute-start(f32[1,32,128]{2,1,0:T(8,128)S(1)} %get-tuple-element.169), channel_id=1, source_target_pairs={{0,4},{4,8},{8,12},{12,16},{16,20},{20,24},{24,28},{28,32},{32,36}... | collective-permute-start | bytes 49160 | tf_op jit(solution)/shard_map/ppermute | solution.py:22
  4.5 8.7 %collective-permute-start = (f32[1,32,128]{2,1,0:T(8,128)S(1)}, f32[1,32,128]{2,1,0:T(8,128)S(1)}, u32[]{:S(2)}, u32[]{:S(2)}) collective-permute-start(f32[1,32,128]{2,1,0:T(8,128)S(1)} %get-tuple-element.168), channel_id=1, source_target_pairs={{4,0},{8,4},{12,8},{16,12},{20,16},{24,20},{28,24},{32,28},{36,32}... | collective-permute-start | bytes 49160 | tf_op jit(solution)/shard_map/ppermute | solution.py:25
  6.7 22.9 %copy-start = (f32[3,16,32,128]{3,2,1,0:T(8,128)S(1)}, f32[3,16,32,128]{3,2,1,0:T(8,128)}, u32[]{:S(2)}) copy-start(f32[3,16,32,128]{3,2,1,0:T(8,128)} %param.8) | copy-start | bytes 2359300
  13.2 13.7 %collective-permute-start.2 = (f32[18,1,128]{2,1,0:T(1,128)S(1)}, f32[18,1,128]{2,1,0:T(1,128)S(1)}, u32[]{:S(2)}, u32[]{:S(2)}) collective-permute-start(f32[18,1,128]{2,1,0:T(1,128)S(1)} %get-tuple-element.167), channel_id=1, source_target_pairs={{1,0},{2,1},{3,2},{5,4},{6,5},{7,6},{9,8},{10,9},{11,10},{13,12},{... | collective-permute-start | bytes 27656 | tf_op jit(solution)/shard_map/ppermute | solution.py:25
  17.2 10.4 %collective-permute-start.3 = (f32[18,1,128]{2,1,0:T(1,128)S(1)}, f32[18,1,128]{2,1,0:T(1,128)S(1)}, u32[]{:S(2)}, u32[]{:S(2)}) collective-permute-start(f32[18,1,128]{2,1,0:T(1,128)S(1)} %get-tuple-element.166), channel_id=1, source_target_pairs={{0,1},{1,2},{2,3},{4,5},{5,6},{6,7},{8,9},{9,10},{10,11},{12,13},{... | collective-permute-start | bytes 27656 | tf_op jit(solution)/shard_map/ppermute | solution.py:22
  29.7 9.5 %collective-permute-start.4 = (f32[3,1,32,128]{3,2,1,0:T(8,128)S(1)}, f32[3,1,32,128]{3,2,1,0:T(8,128)S(1)}, u32[]{:S(2)}, u32[]{:S(2)}) collective-permute-start(f32[3,1,32,128]{3,2,1,0:T(8,128)S(1)} %get-tuple-element.165), channel_id=1, source_target_pairs={{4,0},{8,4},{12,8},{16,12},{20,16},{24,20},{28,24},{32,28},{36,32}... | collective-permute-start | bytes 147464 | tf_op jit(solution)/shard_map/ppermute | solution.py:25
  31.6 8.7 %collective-permute-start.5 = (f32[3,1,32,128]{3,2,1,0:T(8,128)S(1)}, f32[3,1,32,128]{3,2,1,0:T(8,128)S(1)}, u32[]{:S(2)}, u32[]{:S(2)}) collective-permute-start(f32[3,1,32,128]{3,2,1,0:T(8,128)S(1)} %get-tuple-element.164), channel_id=1, source_target_pairs={{0,4},{4,8},{8,12},{12,16},{16,20},{20,24},{24,28},{28,32},{32,36}... | collective-permute-start | bytes 147464 | tf_op jit(solution)/shard_map/ppermute | solution.py:22
  40.4 11.2 %collective-permute-start.6 = (f32[3,18,1,128]{3,2,1,0:T(1,128)S(1)}, f32[3,18,1,128]{3,2,1,0:T(1,128)S(1)}, u32[]{:S(2)}, u32[]{:S(2)}) collective-permute-start(f32[3,18,1,128]{3,2,1,0:T(1,128)S(1)} %get-tuple-element.157), channel_id=1, source_target_pairs={{1,0},{2,1},{3,2},{5,4},{6,5},{7,6},{9,8},{10,9},{11,10},{13,12},{... | collective-permute-start | bytes 82952 | tf_op jit(solution)/shard_map/ppermute | solution.py:25
  42.4 10.2 %collective-permute-start.7 = (f32[3,18,1,128]{3,2,1,0:T(1,128)S(1)}, f32[3,18,1,128]{3,2,1,0:T(1,128)S(1)}, u32[]{:S(2)}, u32[]{:S(2)}) collective-permute-start(f32[3,18,1,128]{3,2,1,0:T(1,128)S(1)} %get-tuple-element.156), channel_id=1, source_target_pairs={{0,1},{1,2},{2,3},{4,5},{5,6},{6,7},{8,9},{9,10},{10,11},{12,13},{... | collective-permute-start | bytes 82952 | tf_op jit(solution)/shard_map/ppermute | solution.py:22
  54.3 10.1 %collective-permute-start.8 = (f32[3,1,32,128]{3,2,1,0:T(8,128)S(1)}, f32[3,1,32,128]{3,2,1,0:T(8,128)S(1)}, u32[]{:S(2)}, u32[]{:S(2)}) collective-permute-start(f32[3,1,32,128]{3,2,1,0:T(8,128)S(1)} %get-tuple-element.163), channel_id=1, source_target_pairs={{4,0},{8,4},{12,8},{16,12},{20,16},{24,20},{28,24},{32,28},{36,32}... | collective-permute-start | bytes 147464 | tf_op jit(solution)/shard_map/ppermute | solution.py:25
  56.2 9.3 %collective-permute-start.9 = (f32[3,1,32,128]{3,2,1,0:T(8,128)S(1)}, f32[3,1,32,128]{3,2,1,0:T(8,128)S(1)}, u32[]{:S(2)}, u32[]{:S(2)}) collective-permute-start(f32[3,1,32,128]{3,2,1,0:T(8,128)S(1)} %get-tuple-element.162), channel_id=1, source_target_pairs={{0,4},{4,8},{8,12},{12,16},{16,20},{20,24},{24,28},{28,32},{32,36}... | collective-permute-start | bytes 147464 | tf_op jit(solution)/shard_map/ppermute | solution.py:22
  65.6 10.9 %collective-permute-start.10 = (f32[3,18,1,128]{3,2,1,0:T(1,128)S(1)}, f32[3,18,1,128]{3,2,1,0:T(1,128)S(1)}, u32[]{:S(2)}, u32[]{:S(2)}) collective-permute-start(f32[3,18,1,128]{3,2,1,0:T(1,128)S(1)} %get-tuple-element.155), channel_id=1, source_target_pairs={{1,0},{2,1},{3,2},{5,4},{6,5},{7,6},{9,8},{10,9},{11,10},{13,12},{... | collective-permute-start | bytes 82952 | tf_op jit(solution)/shard_map/ppermute | solution.py:25
  67.5 9.9 %collective-permute-start.11 = (f32[3,18,1,128]{3,2,1,0:T(1,128)S(1)}, f32[3,18,1,128]{3,2,1,0:T(1,128)S(1)}, u32[]{:S(2)}, u32[]{:S(2)}) collective-permute-start(f32[3,18,1,128]{3,2,1,0:T(1,128)S(1)} %get-tuple-element.154), channel_id=1, source_target_pairs={{0,1},{1,2},{2,3},{4,5},{5,6},{6,7},{8,9},{9,10},{10,11},{12,13},{... | collective-permute-start | bytes 82952 | tf_op jit(solution)/shard_map/ppermute | solution.py:22
  79.2 10.1 %collective-permute-start.12 = (f32[3,1,32,128]{3,2,1,0:T(8,128)S(1)}, f32[3,1,32,128]{3,2,1,0:T(8,128)S(1)}, u32[]{:S(2)}, u32[]{:S(2)}) collective-permute-start(f32[3,1,32,128]{3,2,1,0:T(8,128)S(1)} %get-tuple-element.161), channel_id=1, source_target_pairs={{4,0},{8,4},{12,8},{16,12},{20,16},{24,20},{28,24},{32,28},{36,32}... | collective-permute-start | bytes 147464 | tf_op jit(solution)/shard_map/ppermute | solution.py:25
  81.1 9.3 %collective-permute-start.13 = (f32[3,1,32,128]{3,2,1,0:T(8,128)S(1)}, f32[3,1,32,128]{3,2,1,0:T(8,128)S(1)}, u32[]{:S(2)}, u32[]{:S(2)}) collective-permute-start(f32[3,1,32,128]{3,2,1,0:T(8,128)S(1)} %get-tuple-element.160), channel_id=1, source_target_pairs={{0,4},{4,8},{8,12},{12,16},{16,20},{20,24},{24,28},{28,32},{32,36}... | collective-permute-start | bytes 147464 | tf_op jit(solution)/shard_map/ppermute | solution.py:22
  90.5 10.9 %collective-permute-start.14 = (f32[3,18,1,128]{3,2,1,0:T(1,128)S(1)}, f32[3,18,1,128]{3,2,1,0:T(1,128)S(1)}, u32[]{:S(2)}, u32[]{:S(2)}) collective-permute-start(f32[3,18,1,128]{3,2,1,0:T(1,128)S(1)} %get-tuple-element.153), channel_id=1, source_target_pairs={{1,0},{2,1},{3,2},{5,4},{6,5},{7,6},{9,8},{10,9},{11,10},{13,12},{... | collective-permute-start | bytes 82952 | tf_op jit(solution)/shard_map/ppermute | solution.py:25
  92.5 9.9 %collective-permute-start.15 = (f32[3,18,1,128]{3,2,1,0:T(1,128)S(1)}, f32[3,18,1,128]{3,2,1,0:T(1,128)S(1)}, u32[]{:S(2)}, u32[]{:S(2)}) collective-permute-start(f32[3,18,1,128]{3,2,1,0:T(1,128)S(1)} %get-tuple-element.152), channel_id=1, source_target_pairs={{0,1},{1,2},{2,3},{4,5},{5,6},{6,7},{8,9},{9,10},{10,11},{12,13},{... | collective-permute-start | bytes 82952 | tf_op jit(solution)/shard_map/ppermute | solution.py:22
  103.3 11.0 %copy-start.2 = (s32[1,1,3,1024]{3,1,2,0:T(1,128)S(1)}, s32[1,1,3,1024]{3,1,2,0:T(1,128)}, u32[]{:S(2)}) copy-start(s32[1,1,3,1024]{3,1,2,0:T(1,128)} %param.11) | copy-start | bytes 36868
  104.1 39.7 %copy-start.1 = (f32[3,16,32,128]{3,2,1,0:T(8,128)}, f32[3,16,32,128]{3,2,1,0:T(8,128)S(1)}, u32[]{:S(2)}) copy-start(f32[3,16,32,128]{3,2,1,0:T(8,128)S(1)} %fusion.44) | copy-start | bytes 2359300
  104.2 30.7 %copy-start.3 = (f32[3]{0:T(128)S(1)}, f32[3]{0:T(128)}, u32[]{:S(2)}) copy-start(f32[3]{0:T(128)} %constant.123.clone) | copy-start | bytes 40
  104.2 10.8 %collective-permute-start.16 = (f32[3,4,32,128]{3,2,1,0:T(8,128)S(1)}, f32[3,4,32,128]{3,2,1,0:T(8,128)S(1)}, u32[]{:S(2)}, u32[]{:S(2)}) collective-permute-start(f32[3,4,32,128]{3,2,1,0:T(8,128)S(1)} %get-tuple-element.158), channel_id=1, source_target_pairs={{0,4},{4,8},{8,12},{12,16},{16,20},{20,24},{24,28},{28,32},{32,36}... | collective-permute-start | bytes 589832 | tf_op jit(solution)/shard_map/ppermute | solution.py:22
  112.4 10.9 %collective-permute-start.17 = (f32[3,4,32,128]{3,2,1,0:T(8,128)S(1)}, f32[3,4,32,128]{3,2,1,0:T(8,128)S(1)}, u32[]{:S(2)}, u32[]{:S(2)}) collective-permute-start(f32[3,4,32,128]{3,2,1,0:T(8,128)S(1)} %get-tuple-element.159), channel_id=1, source_target_pairs={{4,0},{8,4},{12,8},{16,12},{20,16},{24,20},{28,24},{32,28},{36,32}... | collective-permute-start | bytes 589832 | tf_op jit(solution)/shard_map/ppermute | solution.py:25
  123.3 12.3 %collective-permute-start.18 = (f32[3,24,4,128]{3,2,1,0:T(4,128)S(1)}, f32[3,24,4,128]{3,2,1,0:T(4,128)S(1)}, u32[]{:S(2)}, u32[]{:S(2)}) collective-permute-start(f32[3,24,4,128]{3,2,1,0:T(4,128)S(1)} %get-tuple-element.150), channel_id=1, source_target_pairs={{0,1},{1,2},{2,3},{4,5},{5,6},{6,7},{8,9},{9,10},{10,11},{12,13},{... | collective-permute-start | bytes 442376 | tf_op jit(solution)/shard_map/ppermute | solution.py:22
  132.7 10.9 %collective-permute-start.19 = (f32[3,24,4,128]{3,2,1,0:T(4,128)S(1)}, f32[3,24,4,128]{3,2,1,0:T(4,128)S(1)}, u32[]{:S(2)}, u32[]{:S(2)}) collective-permute-start(f32[3,24,4,128]{3,2,1,0:T(4,128)S(1)} %get-tuple-element.151), channel_id=1, source_target_pairs={{1,0},{2,1},{3,2},{5,4},{6,5},{7,6},{9,8},{10,9},{11,10},{13,12},{... | collective-permute-start | bytes 442376 | tf_op jit(solution)/shard_map/ppermute | solution.py:25
  157.4 1.4 slice-start
  178.1 1.4 slice-start
  198.8 1.4 slice-start
  219.4 1.4 slice-start
  240.1 1.4 slice-start
  260.8 1.4 slice-start
  281.4 1.4 slice-start
  302.1 1.4 slice-start
where the time goes:
time: 313 us; the launch traced here: 310 us
  starting transfers between devices  103 us (33%)
  local copies, waits for them, and re-layouts  81.7 us (26%)
  other arithmetic  51.4 us (16%)
  matrix products  41.5 us (13%)
  waiting for transfers between devices  29.4 us (9%)
    ppermute x10, starting transfers between devices, extended_2(): lax.ppermute(lax.slice_in_dim(block, block.shape[dim] - width, None, axis...  81.5 us
    reshape x8, local copies, waits for them, and re-layouts, one_block(): jnp.dot(flat, wz, precision=highest).reshape(3, length_x, length_y, 3, 128)  60.3 us
    while x40, other arithmetic  42.2 us
    dot_general x8, matrix products, one_block(): jnp.dot(flat, wz, precision=highest).reshape(3, length_x, length_y, 3, 128)  41.5 us
    ppermute x10, waiting for transfers between devices, extended_2(): lax.ppermute(lax.slice_in_dim(block, 0, width, axis=dim), axis, backward)  21.7 us
    ppermute x10, starting transfers between devices, extended_2(): lax.ppermute(lax.slice_in_dim(block, 0, width, axis=dim), axis, backward)  21.7 us
    slice x16, local copies, waits for them, and re-layouts, one_block(): slope = jnp.einsum('ixyp,yp->ixp', zed[:, :, :, 0], wy1, precision=highest)  10.2 us
    ppermute x10, waiting for transfers between devices, extended_2(): lax.ppermute(lax.slice_in_dim(block, block.shape[dim] - width, None, axis...  7.68 us
  transfers between devices with their start and end apart: 20, of which 11 were waited for; matrix products, arithmetic and copies ran while one was open for 0% of the time, Pallas kernels for 0%

commit v1 on v0

v1 whole, which is shorter than its diff:
```python
import functools
import math

import jax
import jax.numpy as jnp
from jax import lax
from jax.experimental import pallas as pl
from jax.experimental.pallas import tpu as pltpu
from jax.sharding import PartitionSpec as P

MESH = pl.DeviceIdType.MESH
F32 = jnp.float32
BF16 = jnp.bfloat16

RADIUS = 4
CX, CY, NZ = 16, 32, 128
SLOTS = 1024
BLOCKS = SLOTS // 128
HU = 3
HC = 4
XU = CX + 2 * HU
XC = CX + 2 * HC
XW = CX + 2 * RADIUS
YA = 8
YN = CY + 8
Y0 = YA + 4
YB = YN + 16
TILES = YN // 8
KZ = 3 * NZ

WIDTH = 1.25
RELAX = 0.8

DIRS = [(dx, dy) for dx in (-1, 0, 1) for dy in (-1, 0, 1) if (dx, dy) != (0, 0)]


def profile(distance):
    width_sq = WIDTH * WIDTH
    base = jnp.exp(-distance * distance / (2.0 * width_sq)) / (WIDTH * math.sqrt(2.0 * math.pi))
    first = -distance / width_sq * base
    second = (distance * distance / width_sq - 1.0) / width_sq * base
    return (base, first, second)


def weights(places, centre, offset):
    distance = places - centre
    inside = jnp.abs(distance) <= RADIUS
    return [jnp.where(inside, item, 0.0) for item in profile(distance + 0.5 - offset)]


def split(value):
    high = value.astype(BF16)
    return high, (value - high.astype(F32)).astype(BF16)


def along(d, low, own, high):
    return (low, own, high)[d + 1]


def kernel(
    nw, nn, u_ref, k_ref, count_ref, cell_ref, off_ref, out_ref, grad_ref,
    ub, cb, w1, wa, wb, ck, xh, yh, fm, fx, fy, wz, wy, wx,
    own_sem, send_sem, recv_sem, cross_sem,
):
    a, b = lax.axis_index("wide"), lax.axis_index("narrow")
    half = nn // 2

    def exists(d):
        return (a + d[0] >= 0) & (a + d[0] < nw) & (b + d[1] >= 0) & (b + d[1] < nn)

    def same(d):
        if d[1] == 0:
            return exists(d)
        return exists(d) & ((b < half) == (b + d[1] < half))

    def cross(d):
        if d[1] == 0:
            return None
        return exists(d) & ((b < half) != (b + d[1] < half))

    def each(test, action):
        for i, d in enumerate(DIRS):
            ok = test(d)
            if ok is not None:
                pl.when(ok)(functools.partial(action, i, d))

    def number(test):
        return sum(jnp.where(test(d), 1, 0) for d in DIRS if test(d) is not None)

    def copy_of(k, i, d):
        x, y = d
        to = (a + x, b + y)

        def remote(k, src, dst):
            return pltpu.make_async_remote_copy(
                src_ref=src, dst_ref=dst, send_sem=send_sem.at[k, i], recv_sem=recv_sem.at[k, i],
                device_id=to, device_id_type=MESH,
            )

        def parts(n, lo_x, lo_y):
            src = (
                along(x, pl.ds(0, n), pl.ds(0, CX), pl.ds(CX - n, n)),
                along(y, pl.ds(0, n), pl.ds(0, CY), pl.ds(CY - n, n)),
            )
            dst = (
                along(x, pl.ds(lo_x + CX, n), pl.ds(lo_x, CX), pl.ds(lo_x - n, n)),
                along(y, pl.ds(lo_y + CY, n), pl.ds(lo_y, CY), pl.ds(lo_y - n, n)),
            )
            return src, dst

        if k == 0:
            src, dst = parts(HC, HC, Y0)
            return remote(k, k_ref.at[src], cb.at[dst])
        if k == 1:
            src, dst = parts(HU, HU, Y0)
            return remote(k, u_ref.at[:, src[0], src[1]], ub.at[:, dst[0], dst[1]])
        src, _ = parts(RADIUS, RADIUS, RADIUS)
        if x == 0:
            target = yh.at[:, :, along(y, pl.ds(4, 4), None, pl.ds(0, 4))]
        else:
            rows = along(y, pl.ds(CY + 4, 4), pl.ds(4, CY), pl.ds(0, 4))
            target = xh.at[:, along(x, pl.ds(4, 4), None, pl.ds(0, 4)), rows]
        return remote(k, out_ref.at[:, src[0], src[1]], target)

    barrier = pltpu.get_barrier_semaphore()

    def signal(semaphore):
        def action(i, d):
            pl.semaphore_signal(semaphore, inc=1, device_id=(a + d[0], b + d[1]), device_id_type=MESH)

        return action

    def send(i, d):
        for k in range(2):
            copy_of(k, i, d).start()

    each(same, signal(barrier))

    @pl.when(b < half)
    def _():
        each(cross, signal(barrier))

    own_k = pltpu.make_async_copy(k_ref, cb.at[pl.ds(HC, CX), pl.ds(Y0, CY)], own_sem.at[0])
    own_u = pltpu.make_async_copy(u_ref, ub.at[:, pl.ds(HU, CX), pl.ds(Y0, CY)], own_sem.at[1])
    own_k.start()
    own_u.start()

    @pl.when(a == 0)
    def _():
        ub[:, 0:HU] = jnp.zeros((3, HU, YB, NZ), F32)
        cb[0:HC] = jnp.zeros((HC, YB, NZ), F32)
        xh[:, 0:4] = jnp.zeros((3, 4, YN, NZ), F32)

    @pl.when(a == nw - 1)
    def _():
        ub[:, HU + CX :] = jnp.zeros((3, HU, YB, NZ), F32)
        cb[HC + CX :] = jnp.zeros((HC, YB, NZ), F32)
        xh[:, 4:8] = jnp.zeros((3, 4, YN, NZ), F32)

    @pl.when(b == 0)
    def _():
        ub[:, :, Y0 - 4 : Y0] = jnp.zeros((3, XU, 4, NZ), F32)
        cb[:, Y0 - 4 : Y0] = jnp.zeros((XC, 4, NZ), F32)
        xh[:, :, 0:4] = jnp.zeros((3, 8, 4, NZ), F32)
        yh[:, :, 0:4] = jnp.zeros((3, CX, 4, NZ), F32)

    @pl.when(b == nn - 1)
    def _():
        ub[:, :, Y0 + CY : Y0 + CY + 4] = jnp.zeros((3, XU, 4, NZ), F32)
        cb[:, Y0 + CY : Y0 + CY + 4] = jnp.zeros((XC, 4, NZ), F32)
        xh[:, :, CY + 4 :] = jnp.zeros((3, 8, 4, NZ), F32)
        yh[:, :, 4:8] = jnp.zeros((3, CX, 4, NZ), F32)

    @pl.when(b < half)
    def _():
        pl.semaphore_wait(barrier, number(same))
        each(same, send)

    @pl.when(b >= half)
    def _():
        pl.semaphore_wait(barrier, number(exists))
        each(cross, signal(cross_sem))
        each(cross, send)
        each(same, send)

    slot = lax.broadcasted_iota(jnp.int32, (1, 128), 1)

    def prepare(blk, carry):
        centre = [cell_ref[pl.ds(d * BLOCKS + blk, 1)].astype(F32) for d in range(3)]
        offset = [off_ref[pl.ds(d * BLOCKS + blk, 1)] for d in range(3)]
        live = jnp.where(slot + blk * 128 < count_ref[0, 0], 1.0, 0.0)
        rows = lax.broadcasted_iota(jnp.int32, (NZ, 128), 0).astype(F32)
        for i, item in enumerate(weights(rows, centre[2], offset[2])):
            high, low = split(item)
            wz[blk, 0:128, i * 128 : i * 128 + 128] = high
            wz[blk, 128:256, i * 128 : i * 128 + 128] = high
            wz[blk, 256:384, i * 128 : i * 128 + 128] = low
        rows = lax.broadcasted_iota(jnp.int32, (CY + YN + 8, 128), 0)
        tail = rows - CY - YN
        rows = jnp.where(rows < CY, rows, jnp.where(tail < 0, rows - CY - 4, jnp.where(tail < 4, tail - 4, tail + CY - 4)))
        for i, item in enumerate(weights(rows.astype(F32), centre[1], offset[1])):
            wy[blk, i] = item
        rows = lax.broadcasted_iota(jnp.int32, (XW, 128), 0).astype(F32) - RADIUS
        for i, item in enumerate(weights(rows, centre[0], offset[0])):
            wx[blk, i] = item * live
        return carry

    lax.fori_loop(0, BLOCKS, prepare, 0)

    @pl.when(b < half)
    def _():
        @pl.when(b == half - 1)
        def _():
            pl.semaphore_wait(cross_sem, number(cross))

        each(cross, send)

    own_k.wait()
    own_u.wait()

    def arrived(kinds):
        def action(i, d):
            j = DIRS.index((-d[0], -d[1]))
            for k in kinds:
                copy_of(k, j, DIRS[j]).wait_recv()

        return action

    each(exists, arrived((0, 1)))

    lane = lax.broadcasted_iota(jnp.int32, (8, NZ), 1)
    last_z, first_z = lane == NZ - 1, lane == 0
    y_at = lax.broadcasted_iota(jnp.int32, (8, NZ), 0) + (b * CY - 4)

    def face_coefficients(x, carry):
        x_at = a * CX - HU + x
        x_in = (x_at >= 0) & (x_at < nw * CX)
        for t in range(TILES):
            r = YA + 8 * t
            mid = cb[x + 1, r : r + 8]
            beside = [
                cb[x + 2, r : r + 8],
                cb[x, r : r + 8],
                cb[x + 1, r + 1 : r + 9],
                cb[x + 1, r - 1 : r + 7],
                jnp.where(last_z, 0.0, pltpu.roll(mid, NZ - 1, 1)),
                jnp.where(first_z, 0.0, pltpu.roll(mid, 1, 1)),
            ]
            faces = [0.5 * (mid + item) for item in beside]
            total = 1.0 + sum(faces)
            y = y_at + 8 * t
            scale = jnp.where((y >= 0) & (y < nn * CY) & x_in, RELAX / total, 0.0)
            faces[4] = jnp.where(last_z, 0.0, faces[4])
            faces[5] = jnp.where(first_z, 0.0, faces[5])
            for i, face in enumerate(faces):
                ck[i, x, 8 * t : 8 * t + 8] = scale * face
            for c in range(3):
                w1[c, x, r : r + 8] = scale * ub[c, x, r : r + 8]
        return carry

    lax.fori_loop(0, XU, face_coefficients, 0, unroll=2)

    def relaxed(src, x):
        values = [[], [], []]
        for t in range(TILES):
            r = YA + 8 * t
            k = [ck[i, x, 8 * t : 8 * t + 8] for i in range(6)]
            for c in range(3):
                mid = src[c, x, r : r + 8]
                total = (1.0 - RELAX) * mid + w1[c, x, r : r + 8]
                ends = k[4] * pltpu.roll(mid, NZ - 1, 1) + k[5] * pltpu.roll(mid, 1, 1)
                sides = k[2] * src[c, x, r + 1 : r + 9] + k[3] * src[c, x, r - 1 : r + 7]
                total += k[0] * src[c, x + 1, r : r + 8] + k[1] * src[c, x - 1, r : r + 8]
                values[c].append(total + sides + ends)
        return values

    def sweep(src, dst):
        def step(x, carry):
            values = relaxed(src, x)
            for c in range(3):
                for t in range(TILES):
                    dst[c, x, YA + 8 * t : YA + 8 * t + 8] = values[c][t]
            return carry

        return step

    lax.fori_loop(1, XU - 1, sweep(w1, wa), 0, unroll=2)
    lax.fori_loop(2, XU - 2, sweep(wa, wb), 0, unroll=2)

    def store_split(ref, index, value):
        high, low = split(value)
        ref[(*index, slice(0, 128))] = high
        ref[(*index, slice(128, 256))] = low
        ref[(*index, slice(256, 384))] = high

    def last(x, carry):
        values = relaxed(wb, x)
        for c in range(3):
            out_ref[c, x - HU] = jnp.concatenate(values[c], axis=0)[4 : 4 + CY]
        return carry

    lax.fori_loop(HU, HU + CX, last, 0, unroll=2)

    def send_field(i, d):
        copy_of(2, i, d).start()

    each(cross, send_field)
    each(same, send_field)

    def split_own(x, carry):
        for c in range(3):
            store_split(fm, (c, x, slice(None)), out_ref[c, x])
        return carry

    lax.fori_loop(0, CX, split_own, 0, unroll=2)

    def moments(blk, parts, first):
        weight = wz[blk]
        for c in range(3):
            sums = [jnp.zeros((8, 128), F32) for _ in range(4)]
            for ref, tiles, lead, xs in parts:
                field = ref[c] if len(ref.shape) == 3 else ref[c].reshape(CX * CY, KZ)
                product = jnp.dot(field, weight, preferred_element_type=F32)
                for n, x in enumerate(xs):
                    along0 = along1 = slope = bend = None
                    for t in range(tiles):
                        row = (n * tiles + t) * 8
                        t0, t1, t2 = [product[row : row + 8, i * 128 : i * 128 + 128] for i in range(3)]
                        g0, g1, g2 = [wy[blk, i, (lead + t) * 8 : (lead + t) * 8 + 8] for i in range(3)]
                        terms = t0 * g0, t1 * g0, t0 * g1, t0 * g2 + t2 * g0
                        if t == 0:
                            along0, along1, slope, bend = terms
                        else:
                            along0, along1, slope, bend = [p + q for p, q in zip((along0, along1, slope, bend), terms)]
                    x0, x1, x2 = [wx[blk, i, x : x + 1] for i in range(3)]
                    sums[0] += along0 * x1
                    sums[1] += slope * x0
                    sums[2] += along1 * x0
                    sums[3] += along0 * x2 + bend * x0
            for j, item in enumerate(sums):
                at = pl.ds((4 * c + j) * BLOCKS + blk, 1)
                item = jnp.sum(item, axis=0, keepdims=True)
                grad_ref[at] = item if first else grad_ref[at] + item

    def own_moments(blk, carry):
        moments(blk, ((fm, CY // 8, 0, range(4, 4 + CX)),), True)
        return carry

    lax.fori_loop(0, BLOCKS, own_moments, 0)

    each(exists, arrived((2,)))

    for c in range(3):
        store_split(fx, (c, slice(None)), xh[c].reshape(8 * YN, NZ))
        store_split(fy, (c, slice(None)), yh[c].reshape(8 * CX, NZ))

    def halo_moments(blk, carry):
        parts = (
            (fx, YN // 8, CY // 8, (*range(4), *range(20, 24))),
            (fy, 1, (CY + YN) // 8, range(4, 4 + CX)),
        )
        moments(blk, parts, False)
        return carry

    lax.fori_loop(0, BLOCKS, halo_moments, 0)

    def sent(i, d):
        for k in range(3):
            copy_of(k, i, d).wait_send()

    each(exists, sent)


def body(adjoint_velocity, coefficient, record_counts, record_cells, record_offsets):
    nw, nn = lax.axis_size("wide"), lax.axis_size("narrow")
    vmem = pl.BlockSpec(memory_space=pltpu.VMEM)
    hbm = pl.BlockSpec(memory_space=pltpu.HBM)
    smoothed, grads = pl.pallas_call(
        functools.partial(kernel, nw, nn),
        out_shape=(
            jax.ShapeDtypeStruct((3, CX, CY, NZ), F32),
            jax.ShapeDtypeStruct((12 * BLOCKS, 128), F32),
        ),
        in_specs=[hbm, hbm, pl.BlockSpec(memory_space=pltpu.SMEM), vmem, vmem],
        out_specs=(vmem, vmem),
        scratch_shapes=[
            pltpu.VMEM((3, XU, YB, NZ), F32),
            pltpu.VMEM((XC, YB, NZ), F32),
            pltpu.VMEM((3, XU, YB, NZ), F32),
            pltpu.VMEM((3, XU, YB, NZ), F32),
            pltpu.VMEM((3, XU, YB, NZ), F32),
            pltpu.VMEM((6, XU, YN, NZ), F32),
            pltpu.VMEM((3, 8, YN, NZ), F32),
            pltpu.VMEM((3, CX, 8, NZ), F32),
            pltpu.VMEM((3, CX, CY, KZ), BF16),
            pltpu.VMEM((3, 8 * YN, KZ), BF16),
            pltpu.VMEM((3, 8 * CX, KZ), BF16),
            pltpu.VMEM((BLOCKS, KZ, 384), BF16),
            pltpu.VMEM((BLOCKS, 3, CY + YN + 8, 128), F32),
            pltpu.VMEM((BLOCKS, 3, XW, 128), F32),
            pltpu.SemaphoreType.DMA((2,)),
            pltpu.SemaphoreType.DMA((3, 8)),
            pltpu.SemaphoreType.DMA((3, 8)),
            pltpu.SemaphoreType.REGULAR,
        ],
        compiler_params=pltpu.CompilerParams(
            collective_id=0, has_side_effects=True, vmem_limit_bytes=40 << 20
        ),
    )(
        adjoint_velocity,
        coefficient,
        record_counts,
        record_cells.reshape(3 * BLOCKS, 128),
        record_offsets.reshape(3 * BLOCKS, 128),
    )
    return smoothed, grads.reshape(1, 1, 12, SLOTS)


def solution(mesh):
    return jax.shard_map(
        body,
        mesh=mesh,
        in_specs=(
            P(None, "wide", "narrow", None),
            P("wide", "narrow", None),
            P("wide", "narrow"),
            P("wide", "narrow", None, None),
            P("wide", "narrow", None, None),
        ),
        out_specs=(P(None, "wide", "narrow", None), P("wide", "narrow", None, None)),
        check_vma=False,
    )
```

time: 313 us -> 48.3 us (0.15)
  the two profiles are of different devices: /device:TPU:63 before, /device:TPU:123 now
where the time goes in v1:
time: 48.3 us; the launch traced here: 48 us
  Pallas kernels  41.8 us (87%)
  local copies, waits for them, and re-layouts  4.99 us (10%)
  between operations  1.3 us (3%)
    pallas_call x1, Pallas kernels, body(): pl.pallas_call(functools.partial(kernel, nw, nn), out_shape=(jax.ShapeDty...  41.8 us
    unnamed x10, local copies, waits for them, and re-layouts  4.99 us

profile of v1, /device:TPU:123, one launch (start us, length us, event | category | flops | bytes accessed | tf_op | source)
XLA Modules:
  0.0 48.0 jit_solution(2040035978850244487)
XLA Ops:
  1.3 0.0 copy-start
  1.3 1.1 %copy-done = f32[3,16,32,128]{3,2,1,0:T(8,128)S(1)} copy-done((f32[3,16,32,128]{3,2,1,0:T(8,128)S(1)}, f32[3,16,32,128]{3,2,1,0:T(8,128)}, u32[]{:S(2)}) %copy-start) | copy-done | bytes 786456
  2.4 0.0 copy-start.1
  2.4 0.9 %copy-done.1 = f32[16,32,128]{2,1,0:T(8,128)S(1)} copy-done((f32[16,32,128]{2,1,0:T(8,128)S(1)}, f32[16,32,128]{2,1,0:T(8,128)}, u32[]{:S(2)}) %copy-start.1) | copy-done | bytes 262168
  3.4 0.0 copy-start.2
  3.4 0.7 %copy-done.2 = s32[1,1,3,1024]{3,1,2,0:T(1,128)S(1)} copy-done((s32[1,1,3,1024]{3,1,2,0:T(1,128)S(1)}, s32[1,1,3,1024]{3,1,2,0:T(1,128)}, u32[]{:S(2)}) %copy-start.2) | copy-done | bytes 12312
  4.1 0.0 copy-start.3
  4.1 0.7 %copy-done.3 = f32[1,1,3,1024]{3,1,2,0:T(1,128)S(1)} copy-done((f32[1,1,3,1024]{3,1,2,0:T(1,128)S(1)}, f32[1,1,3,1024]{3,1,2,0:T(1,128)}, u32[]{:S(2)}) %copy-start.3) | copy-done | bytes 12312
  4.8 41.8 %shard_map.68 = (f32[3,16,32,128]{3,2,1,0:T(8,128)S(1)}, f32[96,128]{1,0:T(8,128)S(1)}) custom-call(f32[3,16,32,128]{3,2,1,0:T(8,128)S(1)} %copy-done, f32[16,32,128]{2,1,0:T(8,128)S(1)} %copy-done.1, s32[1,1]{1,0:T(1,128)S(6)} %copy.11.count_ref, s32[24,128]{1,0:T(8,128)S(1)} %bitcast.4, f32[24,128]{1,0:T(8,128)S(1)} %bitcast.5), custom_call_target="tpu_custom_call" | custom-call | tf_op jit(solution)/shard_map/pallas_call | solution.py:378
  46.5 0.9 %copy.12 = f32[3,16,32,128]{3,2,1,0:T(8,128)} copy(f32[3,16,32,128]{3,2,1,0:T(8,128)S(1)} %get-tuple-element.12) | data formatting | bytes 1572864
  47.4 0.6 %copy.13 = f32[1,1,12,1024]{3,1,2,0:T(1,128)} copy(f32[1,1,12,1024]{3,1,2,0:T(1,128)S(1)} %bitcast.3) | data formatting | bytes 98304
Async XLA Ops:
  1.3 1.1 %copy-start = (f32[3,16,32,128]{3,2,1,0:T(8,128)S(1)}, f32[3,16,32,128]{3,2,1,0:T(8,128)}, u32[]{:S(2)}) copy-start(f32[3,16,32,128]{3,2,1,0:T(8,128)} %u_ref.1) | copy-start | bytes 2359300
  2.4 0.9 %copy-start.1 = (f32[16,32,128]{2,1,0:T(8,128)S(1)}, f32[16,32,128]{2,1,0:T(8,128)}, u32[]{:S(2)}) copy-start(f32[16,32,128]{2,1,0:T(8,128)} %k_ref.1) | copy-start | bytes 786436
  3.4 0.7 %copy-start.2 = (s32[1,1,3,1024]{3,1,2,0:T(1,128)S(1)}, s32[1,1,3,1024]{3,1,2,0:T(1,128)}, u32[]{:S(2)}) copy-start(s32[1,1,3,1024]{3,1,2,0:T(1,128)} %param.8) | copy-start | bytes 36868
  4.1 0.7 %copy-start.3 = (f32[1,1,3,1024]{3,1,2,0:T(1,128)S(1)}, f32[1,1,3,1024]{3,1,2,0:T(1,128)}, u32[]{:S(2)}) copy-start(f32[1,1,3,1024]{3,1,2,0:T(1,128)} %param.9) | copy-start | bytes 36868

commit v2 on v1

v2 whole, which is shorter than its diff:
```python
import functools
import math

import jax
import jax.numpy as jnp
from jax import lax
from jax.experimental import pallas as pl
from jax.experimental.pallas import tpu as pltpu
from jax.sharding import PartitionSpec as P

MESH = pl.DeviceIdType.MESH
F32 = jnp.float32
BF16 = jnp.bfloat16

RADIUS = 4
CX, CY, NZ = 16, 32, 128
SLOTS = 1024
BLOCKS = SLOTS // 128
HU = 3
HC = 4
XU = CX + 2 * HU
XC = CX + 2 * HC
YA = 8
YN = CY + 8
Y0 = YA + 4
YB = YN + 16
TILES = YN // 8
KZ = 3 * NZ
FOREIGN = 7
PACKED = FOREIGN * 128
CLASSES = (
    ((-1, 0), 0, 256),
    ((1, 0), 256, 256),
    ((0, -1), 512, 128),
    ((0, 1), 640, 128),
    ((-1, -1), 768, 32),
    ((-1, 1), 800, 32),
    ((1, -1), 832, 32),
    ((1, 1), 864, 32),
)
CORNERS = ((-1, -1), (-1, 1), (1, -1), (1, 1))

WIDTH = 1.25
RELAX = 0.8

DIRS = [(dx, dy) for dx in (-1, 0, 1) for dy in (-1, 0, 1) if (dx, dy) != (0, 0)]


def profile(distance):
    width_sq = WIDTH * WIDTH
    base = jnp.exp(-distance * distance / (2.0 * width_sq)) / (WIDTH * math.sqrt(2.0 * math.pi))
    first = -distance / width_sq * base
    second = (distance * distance / width_sq - 1.0) / width_sq * base
    return (base, first, second)


def weights(places, centre, offset):
    distance = places - centre
    inside = jnp.abs(distance) <= RADIUS
    return [jnp.where(inside, item, 0.0) for item in profile(distance + 0.5 - offset)]


def split(value):
    high = value.astype(BF16)
    return high, (value - high.astype(F32)).astype(BF16)


def blocks_of(d, landing):
    if d[0] and d[1]:
        return pl.ds(6 + (CORNERS.index(d) if landing else 0), 1)
    return {(-1, 0): pl.ds(0, 2), (1, 0): pl.ds(2, 2), (0, -1): pl.ds(4, 1), (0, 1): pl.ds(5, 1)}[d]


def along(d, low, own, high):
    return (low, own, high)[d + 1]


def kernel(
    nw, nn, u_ref, k_ref, count_ref, cell_ref, off_ref, out_ref, grad_ref,
    ub, cb, w1, wa, wb, ck, fm, fe, wz, wy, wx, gm, dm, mine, theirs, part, back, total,
    own_sem, send_sem, recv_sem,
):
    a, b = lax.axis_index("wide"), lax.axis_index("narrow")
    half = nn // 2

    def exists(d):
        return (a + d[0] >= 0) & (a + d[0] < nw) & (b + d[1] >= 0) & (b + d[1] < nn)

    def same(d):
        if d[1] == 0:
            return exists(d)
        return exists(d) & ((b < half) == (b + d[1] < half))

    def cross(d):
        if d[1] == 0:
            return None
        return exists(d) & ((b < half) != (b + d[1] < half))

    def each(test, action):
        for i, d in enumerate(DIRS):
            ok = test(d)
            if ok is not None:
                pl.when(ok)(functools.partial(action, i, d))

    def number(test):
        return sum(jnp.where(test(d), 1, 0) for d in DIRS if test(d) is not None)

    def copy_of(k, i, d):
        x, y = d
        to = (a + x, b + y)

        def remote(k, src, dst):
            return pltpu.make_async_remote_copy(
                src_ref=src, dst_ref=dst, send_sem=send_sem.at[k, i], recv_sem=recv_sem.at[k, i],
                device_id=to, device_id_type=MESH,
            )

        def parts(n, lo_x, lo_y):
            src = (
                along(x, pl.ds(0, n), pl.ds(0, CX), pl.ds(CX - n, n)),
                along(y, pl.ds(0, n), pl.ds(0, CY), pl.ds(CY - n, n)),
            )
            dst = (
                along(x, pl.ds(lo_x + CX, n), pl.ds(lo_x, CX), pl.ds(lo_x - n, n)),
                along(y, pl.ds(lo_y + CY, n), pl.ds(lo_y, CY), pl.ds(lo_y - n, n)),
            )
            return src, dst

        if k == 0:
            src, dst = parts(HC, HC, Y0)
            return remote(k, k_ref.at[src], cb.at[dst])
        if k == 1:
            src, dst = parts(HU, HU, Y0)
            return remote(k, u_ref.at[:, src[0], src[1]], ub.at[:, dst[0], dst[1]])
        if k == 2:
            return remote(k, mine.at[blocks_of(d, False)], theirs.at[blocks_of(d, True)])
        came = (-x, -y)
        return remote(k, part.at[blocks_of(came, False)], back.at[blocks_of(came, True)])

    barrier = pltpu.get_barrier_semaphore()

    def signal(i, d):
        pl.semaphore_signal(barrier, inc=1, device_id=(a + d[0], b + d[1]), device_id_type=MESH)

    def send(i, d):
        for k in range(3):
            copy_of(k, i, d).start()

    each(exists, signal)
    own_k = pltpu.make_async_copy(k_ref, cb.at[pl.ds(HC, CX), pl.ds(Y0, CY)], own_sem.at[0])
    own_u = pltpu.make_async_copy(u_ref, ub.at[:, pl.ds(HU, CX), pl.ds(Y0, CY)], own_sem.at[1])
    own_k.start()
    own_u.start()

    @pl.when(a == 0)
    def _():
        ub[:, 0:HU] = jnp.zeros((3, HU, YB, NZ), F32)
        cb[0:HC] = jnp.zeros((HC, YB, NZ), F32)

    @pl.when(a == nw - 1)
    def _():
        ub[:, HU + CX :] = jnp.zeros((3, HU, YB, NZ), F32)
        cb[HC + CX :] = jnp.zeros((HC, YB, NZ), F32)

    @pl.when(b == 0)
    def _():
        ub[:, :, Y0 - 4 : Y0] = jnp.zeros((3, XU, 4, NZ), F32)
        cb[:, Y0 - 4 : Y0] = jnp.zeros((XC, 4, NZ), F32)

    @pl.when(b == nn - 1)
    def _():
        ub[:, :, Y0 + CY : Y0 + CY + 4] = jnp.zeros((3, XU, 4, NZ), F32)
        cb[:, Y0 + CY : Y0 + CY + 4] = jnp.zeros((XC, 4, NZ), F32)

    for d in DIRS:

        @pl.when(jnp.logical_not(exists(d)))
        def _():
            at, came = blocks_of(d, True), blocks_of((-d[0], -d[1]), True)
            back[at] = jnp.zeros((at.size, 16, 128), F32)
            theirs[came] = jnp.zeros((came.size, 8, 128), F32)

    lane1 = lax.broadcasted_iota(jnp.int32, (1, 128), 1)
    before = lax.broadcasted_iota(jnp.int32, (128, 128), 0) < lax.broadcasted_iota(jnp.int32, (128, 128), 1)
    before = jnp.where(before, 1.0, 0.0).astype(BF16)
    starts = jnp.concatenate([jnp.full((1, 128), first, F32) for _, first, _ in CLASSES], axis=0)

    def record(blk):
        centre = [cell_ref[pl.ds(d * BLOCKS + blk, 1)].astype(F32) for d in range(3)]
        offset = [off_ref[pl.ds(d * BLOCKS + blk, 1)] for d in range(3)]
        live = jnp.where(lane1 + blk * 128 < count_ref[0, 0], 1.0, 0.0)
        return centre, offset, live

    def pack(blk, seen):
        lanes = pl.ds(pl.multiple_of(blk * 128, 128), 128)
        centre, offset, live = record(blk)
        reach = {
            (0, -1): centre[0] < RADIUS, (0, 1): centre[0] >= CX - RADIUS,
            (1, -1): centre[1] < RADIUS, (1, 1): centre[1] >= CY - RADIUS,
        }
        member = []
        for d, _, _ in CLASSES:
            one = jnp.ones((1, 128), F32)
            for axis in range(2):
                if d[axis]:
                    one = jnp.where(reach[axis, d[axis]], one, 0.0)
            member.append(one)
        member = jnp.concatenate(member, axis=0)
        place = jnp.dot(member.astype(BF16), before, preferred_element_type=F32) + seen + starts
        place = jnp.where(member > 0.0, place, -1.0)
        for i, (_, first, size) in enumerate(CLASSES):
            rows = lax.broadcasted_iota(jnp.int32, (size, 128), 0).astype(F32) + float(first)
            gm[first : first + size, lanes] = jnp.where(rows == place[i : i + 1], 1.0, 0.0).astype(BF16)
        pieces = list(centre)
        rest = offset
        for _ in range(3):
            high = [item.astype(BF16).astype(F32) for item in rest]
            rest = [item - piece for item, piece in zip(rest, high)]
            pieces += high
        pieces += [live] + [jnp.zeros((1, 128), F32)] * 3
        dm[:, lanes] = jnp.concatenate(pieces, axis=0).astype(BF16)
        return seen + jnp.sum(member, axis=1, keepdims=True)

    lax.fori_loop(0, BLOCKS, pack, jnp.zeros((8, 128), F32))
    packed = lax.dot_general(dm[...], gm[...], (((1,), (1,)), ((), ())), preferred_element_type=F32)
    for f in range(FOREIGN):
        item = packed[:, f * 128 : f * 128 + 128]
        offset = item[3:6] + (item[6:9] + item[9:12])
        mine[f] = jnp.concatenate([item[0:3], offset, item[12:14]], axis=0)

    pl.semaphore_wait(barrier, number(exists))
    each(cross, send)
    each(same, send)

    def prepare(blk, centre, offset, live):
        rows = lax.broadcasted_iota(jnp.int32, (NZ, 128), 0).astype(F32)
        for i, item in enumerate(weights(rows, centre[2], offset[2])):
            high, low = split(item)
            wz[blk, 0:128, i * 128 : i * 128 + 128] = high
            wz[blk, 128:256, i * 128 : i * 128 + 128] = high
            wz[blk, 256:384, i * 128 : i * 128 + 128] = low
        rows = lax.broadcasted_iota(jnp.int32, (CY, 128), 0).astype(F32)
        for i, item in enumerate(weights(rows, centre[1], offset[1])):
            wy[blk, i] = item
        for i, item in enumerate(weights(rows[:CX], centre[0], offset[0])):
            wx[blk, i] = item * live

    def prepare_own(blk, carry):
        prepare(blk, *record(blk))
        return carry

    lax.fori_loop(0, BLOCKS, prepare_own, 0)

    def arrived(k):
        def action(i, d):
            j = DIRS.index((-d[0], -d[1]))
            copy_of(k, j, DIRS[j]).wait_recv()

        return action

    def corner(values):
        result = values[3]
        for i in (2, 1, 0):
            result = jnp.where(lane1 < 32 * (i + 1), values[i], result)
        return result

    each(exists, arrived(2))
    for f in range(FOREIGN):
        if f < 6:
            item = theirs[f]
            dx, dy = ((-1, 0), (-1, 0), (1, 0), (1, 0), (0, -1), (0, 1))[f]
            shift = -float(dx * CX), -float(dy * CY)
        else:
            item = corner([theirs[6 + i] for i in range(4)])
            shift = [corner([jnp.full((1, 128), -float(d[axis] * n), F32) for d in CORNERS]) for axis, n in ((0, CX), (1, CY))]
        centre = [item[0:1] + shift[0], item[1:2] + shift[1], item[2:3]]
        prepare(BLOCKS + f, centre, [item[3:4], item[4:5], item[5:6]], item[6:7])

    own_k.wait()
    own_u.wait()

    each(exists, arrived(0))
    each(exists, arrived(1))

    lane = lax.broadcasted_iota(jnp.int32, (8, NZ), 1)
    last_z, first_z = lane == NZ - 1, lane == 0
    y_at = lax.broadcasted_iota(jnp.int32, (8, NZ), 0) + (b * CY - 4)

    def face_coefficients(x, carry):
        x_at = a * CX - HU + x
        x_in = (x_at >= 0) & (x_at < nw * CX)
        for t in range(TILES):
            r = YA + 8 * t
            mid = cb[x + 1, r : r + 8]
            beside = [
                cb[x + 2, r : r + 8],
                cb[x, r : r + 8],
                cb[x + 1, r + 1 : r + 9],
                cb[x + 1, r - 1 : r + 7],
                jnp.where(last_z, 0.0, pltpu.roll(mid, NZ - 1, 1)),
                jnp.where(first_z, 0.0, pltpu.roll(mid, 1, 1)),
            ]
            faces = [0.5 * (mid + item) for item in beside]
            total = 1.0 + sum(faces)
            y = y_at + 8 * t
            scale = jnp.where((y >= 0) & (y < nn * CY) & x_in, RELAX / total, 0.0)
            faces[4] = jnp.where(last_z, 0.0, faces[4])
            faces[5] = jnp.where(first_z, 0.0, faces[5])
            for i, face in enumerate(faces):
                ck[i, x, 8 * t : 8 * t + 8] = scale * face
            for c in range(3):
                w1[c, x, r : r + 8] = scale * ub[c, x, r : r + 8]
        return carry

    lax.fori_loop(0, XU, face_coefficients, 0, unroll=2)

    def relaxed(src, x):
        values = [[], [], []]
        for t in range(TILES):
            r = YA + 8 * t
            k = [ck[i, x, 8 * t : 8 * t + 8] for i in range(6)]
            for c in range(3):
                mid = src[c, x, r : r + 8]
                total = (1.0 - RELAX) * mid + w1[c, x, r : r + 8]
                ends = k[4] * pltpu.roll(mid, NZ - 1, 1) + k[5] * pltpu.roll(mid, 1, 1)
                sides = k[2] * src[c, x, r + 1 : r + 9] + k[3] * src[c, x, r - 1 : r + 7]
                total += k[0] * src[c, x + 1, r : r + 8] + k[1] * src[c, x - 1, r : r + 8]
                values[c].append(total + sides + ends)
        return values

    def sweep(src, dst):
        def step(x, carry):
            values = relaxed(src, x)
            for c in range(3):
                for t in range(TILES):
                    dst[c, x, YA + 8 * t : YA + 8 * t + 8] = values[c][t]
            return carry

        return step

    lax.fori_loop(1, XU - 1, sweep(w1, wa), 0, unroll=2)
    lax.fori_loop(2, XU - 2, sweep(wa, wb), 0, unroll=2)

    def store_split(ref, index, value):
        high, low = split(value)
        ref[(*index, slice(0, 128))] = high
        ref[(*index, slice(128, 256))] = low
        ref[(*index, slice(256, 384))] = high

    def last(x, carry):
        values = relaxed(wb, x)
        for c in range(3):
            out_ref[c, x - HU] = jnp.concatenate(values[c], axis=0)[4 : 4 + CY]
        return carry

    lax.fori_loop(HU, HU + CX, last, 0, unroll=2)

    def split_own(x, carry):
        for c in range(3):
            field = out_ref[c, x]
            store_split(fm, (c, x, slice(None)), field)
            store_split(fe, (c, x, slice(None)), jnp.concatenate([field[:8], field[CY - 8 :]], axis=0))
        return carry

    lax.fori_loop(0, CX, split_own, 0, unroll=2)

    def contract(blk, product, row, xs, tiles, step):
        sums = [jnp.zeros((8, 128), F32) for _ in range(4)]
        for n, x in enumerate(xs):
            along0 = along1 = slope = bend = None
            for at, t in tiles:
                r = row + (n * step + at) * 8
                t0, t1, t2 = [product[r : r + 8, i * 128 : i * 128 + 128] for i in range(3)]
                g0, g1, g2 = [wy[blk, i, t * 8 : t * 8 + 8] for i in range(3)]
                terms = t0 * g0, t1 * g0, t0 * g1, t0 * g2 + t2 * g0
                if along0 is None:
                    along0, along1, slope, bend = terms
                else:
                    along0, along1, slope, bend = [p + q for p, q in zip((along0, along1, slope, bend), terms)]
            x0, x1, x2 = [wx[blk, i, x : x + 1] for i in range(3)]
            sums[0] += along0 * x1
            sums[1] += slope * x0
            sums[2] += along1 * x0
            sums[3] += along0 * x2 + bend * x0
        return [jnp.sum(item, axis=0, keepdims=True) for item in sums]

    own_tiles = tuple((t, t) for t in range(CY // 8))
    for f in range(FOREIGN):
        blk = BLOCKS + f
        if f < 4:
            xs, tiles, step = range(12, 16) if f < 2 else range(4), own_tiles, CY // 8
            field = fm[:, xs[0] : xs[0] + 4].reshape(3 * 4 * CY, KZ)
        elif f < 6:
            xs, tiles, step = range(CX), (((1, 3),), ((0, 0),))[f - 4], 2
            field = fe[...].reshape(3 * CX * 16, KZ)
        else:
            xs, tiles, step = (*range(4), *range(12, 16)), ((0, 0), (1, 3)), 2
            field = jnp.concatenate([fe[c, x : x + 4].reshape(64, KZ) for c in range(3) for x in (0, 12)], axis=0)
        product = jnp.dot(field, wz[blk], preferred_element_type=F32)
        rows = []
        for c in range(3):
            rows += contract(blk, product, c * len(xs) * step * 8, xs, tiles, step)
        part[f] = jnp.concatenate(rows + [jnp.zeros((4, 128), F32)], axis=0)

    def send_back(i, d):
        copy_of(3, i, d).start()

    each(cross, send_back)
    each(same, send_back)

    def own_moments(blk, carry):
        rows = []
        for c in range(3):
            product = jnp.dot(fm[c].reshape(CX * CY, KZ), wz[blk], preferred_element_type=F32)
            rows += contract(blk, product, 0, range(CX), own_tiles, CY // 8)
        lanes = pl.ds(pl.multiple_of(blk * 128, 128), 128)
        total[:, lanes] = jnp.concatenate(rows + [jnp.zeros((4, 128), F32)], axis=0)
        return carry

    lax.fori_loop(0, BLOCKS, own_moments, 0)

    each(exists, arrived(3))
    high, low = [], []
    for f in range(FOREIGN):
        item = back[f] if f < 6 else corner([back[6 + i] for i in range(4)])
        piece, rest = split(item)
        high.append(piece)
        low.append(rest)
    both = jnp.concatenate([jnp.concatenate(high, axis=1), jnp.concatenate(low, axis=1)], axis=0)
    spread = jnp.dot(both, gm[...], preferred_element_type=F32)
    grad_ref[0, 0] = (total[...] + (spread[:16] + spread[16:]))[:12]

    def sent(i, d):
        for k in range(4):
            copy_of(k, i, d).wait_send()

    each(exists, sent)


def body(adjoint_velocity, coefficient, record_counts, record_cells, record_offsets):
    nw, nn = lax.axis_size("wide"), lax.axis_size("narrow")
    vmem = pl.BlockSpec(memory_space=pltpu.VMEM)
    hbm = pl.BlockSpec(memory_space=pltpu.HBM)
    return pl.pallas_call(
        functools.partial(kernel, nw, nn),
        out_shape=(
            jax.ShapeDtypeStruct((3, CX, CY, NZ), F32),
            jax.ShapeDtypeStruct((1, 1, 12, SLOTS), F32),
        ),
        in_specs=[hbm, hbm, pl.BlockSpec(memory_space=pltpu.SMEM), vmem, vmem],
        out_specs=(vmem, vmem),
        scratch_shapes=[
            pltpu.VMEM((3, XU, YB, NZ), F32),
            pltpu.VMEM((XC, YB, NZ), F32),
            pltpu.VMEM((3, XU, YB, NZ), F32),
            pltpu.VMEM((3, XU, YB, NZ), F32),
            pltpu.VMEM((3, XU, YB, NZ), F32),
            pltpu.VMEM((6, XU, YN, NZ), F32),
            pltpu.VMEM((3, CX, CY, KZ), BF16),
            pltpu.VMEM((3, CX, 16, KZ), BF16),
            pltpu.VMEM((BLOCKS + FOREIGN, KZ, 384), BF16),
            pltpu.VMEM((BLOCKS + FOREIGN, 3, CY, 128), F32),
            pltpu.VMEM((BLOCKS + FOREIGN, 3, CX, 128), F32),
            pltpu.VMEM((PACKED, SLOTS), BF16),
            pltpu.VMEM((16, SLOTS), BF16),
            pltpu.VMEM((FOREIGN, 8, 128), F32),
            pltpu.VMEM((FOREIGN + 3, 8, 128), F32),
            pltpu.VMEM((FOREIGN, 16, 128), F32),
            pltpu.VMEM((FOREIGN + 3, 16, 128), F32),
            pltpu.VMEM((16, SLOTS), F32),
            pltpu.SemaphoreType.DMA((2,)),
            pltpu.SemaphoreType.DMA((4, 8)),
            pltpu.SemaphoreType.DMA((4, 8)),
        ],
        compiler_params=pltpu.CompilerParams(
            collective_id=0, has_side_effects=True, vmem_limit_bytes=40 << 20
        ),
    )(
        adjoint_velocity,
        coefficient,
        record_counts,
        record_cells.reshape(3 * BLOCKS, 128),
        record_offsets.reshape(3 * BLOCKS, 128),
    )


def solution(mesh):
    return jax.shard_map(
        body,
        mesh=mesh,
        in_specs=(
            P(None, "wide", "narrow", None),
            P("wide", "narrow", None),
            P("wide", "narrow"),
            P("wide", "narrow", None, None),
            P("wide", "narrow", None, None),
        ),
        out_specs=(P(None, "wide", "narrow", None), P("wide", "narrow", None, None)),
        check_vma=False,
    )
```

time: 48.3 us -> 44.7 us (0.925)
  Pallas kernels: 41.8 us -> 38.1 us
    pallas_call x1, Pallas kernels: 41.8 us -> 38.1 us  [body(): pl.pallas_call(functools.partial(kernel, nw, nn), out_shape=(jax.ShapeDty...]
    pallas_call x0 -> x1, local copies, waits for them, and re-layouts: none -> 0.67 us  [body(): pl.pallas_call(functools.partial(kernel, nw, nn), out_shape=(jax.ShapeDty...]
    unnamed x10 -> x9, local copies, waits for them, and re-layouts: 4.99 us -> 4.37 us
where the time goes in v2:
time: 44.7 us; the launch traced here: 44.4 us
  Pallas kernels  38.1 us (85%)
  local copies, waits for them, and re-layouts  5.04 us (11%)
  between operations  1.3 us (3%)
    pallas_call x1, Pallas kernels, body(): pl.pallas_call(functools.partial(kernel, nw, nn), out_shape=(jax.ShapeDty...  38.1 us
    unnamed x9, local copies, waits for them, and re-layouts  4.37 us

profile of v2, /device:TPU:123, one launch (start us, length us, event | category | flops | bytes accessed | tf_op | source)
XLA Modules:
  0.0 44.4 jit_solution(2959727432393394937)
XLA Ops:
  1.3 0.0 copy-start
  1.3 1.1 %copy-done = f32[3,16,32,128]{3,2,1,0:T(8,128)S(1)} copy-done((f32[3,16,32,128]{3,2,1,0:T(8,128)S(1)}, f32[3,16,32,128]{3,2,1,0:T(8,128)}, u32[]{:S(2)}) %copy-start) | copy-done | bytes 786456
  2.4 0.0 copy-start.1
  2.4 0.9 %copy-done.1 = f32[16,32,128]{2,1,0:T(8,128)S(1)} copy-done((f32[16,32,128]{2,1,0:T(8,128)S(1)}, f32[16,32,128]{2,1,0:T(8,128)}, u32[]{:S(2)}) %copy-start.1) | copy-done | bytes 262168
  3.4 0.0 copy-start.2
  3.4 0.7 %copy-done.2 = s32[1,1,3,1024]{3,1,2,0:T(1,128)S(1)} copy-done((s32[1,1,3,1024]{3,1,2,0:T(1,128)S(1)}, s32[1,1,3,1024]{3,1,2,0:T(1,128)}, u32[]{:S(2)}) %copy-start.2) | copy-done | bytes 12312
  4.1 0.0 copy-start.3
  4.1 0.7 %copy-done.3 = f32[1,1,3,1024]{3,1,2,0:T(1,128)S(1)} copy-done((f32[1,1,3,1024]{3,1,2,0:T(1,128)S(1)}, f32[1,1,3,1024]{3,1,2,0:T(1,128)}, u32[]{:S(2)}) %copy-start.3) | copy-done | bytes 12312
  4.8 38.1 %shard_map.68 = (f32[3,16,32,128]{3,2,1,0:T(8,128)S(1)}, f32[1,1,12,1024]{3,2,1,0:T(8,128)S(1)}) custom-call(f32[3,16,32,128]{3,2,1,0:T(8,128)S(1)} %copy-done, f32[16,32,128]{2,1,0:T(8,128)S(1)} %copy-done.1, s32[1,1]{1,0:T(1,128)S(6)} %copy.9.count_ref, s32[24,128]{1,0:T(8,128)S(1)} %bitcast.2, f32[24,128]{1,0:T(8,128)S(1)} %bitcast.3), custom_call_target="tpu_custom_call" | custom-call | tf_op jit(solution)/shard_map/pallas_call | solution.py:444
  42.8 0.7 %copy.7 = f32[1,1,12,1024]{3,1,2,0:T(1,128)} copy(f32[1,1,12,1024]{3,2,1,0:T(8,128)S(1)} %get-tuple-element.3) | data formatting | bytes 98304 | tf_op jit(solution)/shard_map/pallas_call | solution.py:444
  43.5 0.9 %copy.10 = f32[3,16,32,128]{3,2,1,0:T(8,128)} copy(f32[3,16,32,128]{3,2,1,0:T(8,128)S(1)} %get-tuple-element.6) | data formatting | bytes 1572864
Async XLA Ops:
  1.3 1.1 %copy-start = (f32[3,16,32,128]{3,2,1,0:T(8,128)S(1)}, f32[3,16,32,128]{3,2,1,0:T(8,128)}, u32[]{:S(2)}) copy-start(f32[3,16,32,128]{3,2,1,0:T(8,128)} %u_ref.1) | copy-start | bytes 2359300
  2.4 0.9 %copy-start.1 = (f32[16,32,128]{2,1,0:T(8,128)S(1)}, f32[16,32,128]{2,1,0:T(8,128)}, u32[]{:S(2)}) copy-start(f32[16,32,128]{2,1,0:T(8,128)} %k_ref.1) | copy-start | bytes 786436
  3.4 0.7 %copy-start.2 = (s32[1,1,3,1024]{3,1,2,0:T(1,128)S(1)}, s32[1,1,3,1024]{3,1,2,0:T(1,128)}, u32[]{:S(2)}) copy-start(s32[1,1,3,1024]{3,1,2,0:T(1,128)} %param.8) | copy-start | bytes 36868
  4.1 0.7 %copy-start.3 = (f32[1,1,3,1024]{3,1,2,0:T(1,128)S(1)}, f32[1,1,3,1024]{3,1,2,0:T(1,128)}, u32[]{:S(2)}) copy-start(f32[1,1,3,1024]{3,1,2,0:T(1,128)} %param.9) | copy-start | bytes 36868

commit v3 on v2

--- a/solution.py
+++ b/solution.py
@@ -76,8 +76,8 @@
 
 
 def kernel(
-    nw, nn, u_ref, k_ref, count_ref, cell_ref, off_ref, out_ref, grad_ref,
-    ub, cb, w1, wa, wb, ck, fm, fe, wz, wy, wx, gm, dm, mine, theirs, part, back, total,
+    nw, nn, u_ref, k_ref, count_ref, cells, offsets, out, grad_ref,
+    ub, cb, w1, wa, wb, ck, fm, fe, wz, wy, wx, gm, dm, mine, theirs, part, back, total, cell_ref, off_ref, out_ref,
     own_sem, send_sem, recv_sem,
 ):
     a, b = lax.axis_index("wide"), lax.axis_index("narrow")
@@ -117,8 +117,8 @@
 
         def parts(n, lo_x, lo_y):
             src = (
-                along(x, pl.ds(0, n), pl.ds(0, CX), pl.ds(CX - n, n)),
-                along(y, pl.ds(0, n), pl.ds(0, CY), pl.ds(CY - n, n)),
+                along(x, pl.ds(lo_x, n), pl.ds(lo_x, CX), pl.ds(lo_x + CX - n, n)),
+                along(y, pl.ds(lo_y, n), pl.ds(lo_y, CY), pl.ds(lo_y + CY - n, n)),
             )
             dst = (
                 along(x, pl.ds(lo_x + CX, n), pl.ds(lo_x, CX), pl.ds(lo_x - n, n)),
@@ -128,10 +128,10 @@
 
         if k == 0:
             src, dst = parts(HC, HC, Y0)
-            return remote(k, k_ref.at[src], cb.at[dst])
+            return remote(k, cb.at[src], cb.at[dst])
         if k == 1:
             src, dst = parts(HU, HU, Y0)
-            return remote(k, u_ref.at[:, src[0], src[1]], ub.at[:, dst[0], dst[1]])
+            return remote(k, ub.at[:, src[0], src[1]], ub.at[:, dst[0], dst[1]])
         if k == 2:
             return remote(k, mine.at[blocks_of(d, False)], theirs.at[blocks_of(d, True)])
         came = (-x, -y)
@@ -149,8 +149,10 @@
     each(exists, signal)
     own_k = pltpu.make_async_copy(k_ref, cb.at[pl.ds(HC, CX), pl.ds(Y0, CY)], own_sem.at[0])
     own_u = pltpu.make_async_copy(u_ref, ub.at[:, pl.ds(HU, CX), pl.ds(Y0, CY)], own_sem.at[1])
-    own_k.start()
-    own_u.start()
+    own_cells = pltpu.make_async_copy(cells, cell_ref, own_sem.at[2])
+    own_offsets = pltpu.make_async_copy(offsets, off_ref, own_sem.at[3])
+    for copy in (own_cells, own_offsets, own_k, own_u):
+        copy.start()
 
     @pl.when(a == 0)
     def _():
@@ -221,6 +223,8 @@
         dm[:, lanes] = jnp.concatenate(pieces, axis=0).astype(BF16)
         return seen + jnp.sum(member, axis=1, keepdims=True)
 
+    own_cells.wait()
+    own_offsets.wait()
     lax.fori_loop(0, BLOCKS, pack, jnp.zeros((8, 128), F32))
     packed = lax.dot_general(dm[...], gm[...], (((1,), (1,)), ((), ())), preferred_element_type=F32)
     for f in range(FOREIGN):
@@ -228,17 +232,23 @@
         offset = item[3:6] + (item[6:9] + item[9:12])
         mine[f] = jnp.concatenate([item[0:3], offset, item[12:14]], axis=0)
 
+    own_k.wait()
+    own_u.wait()
     pl.semaphore_wait(barrier, number(exists))
     each(cross, send)
     each(same, send)
 
     def prepare(blk, centre, offset, live):
+        def at(i):
+            start = blk % 2 * 384 + i * 128
+            return pl.ds(start if isinstance(blk, int) else pl.multiple_of(start, 128), 128)
+
         rows = lax.broadcasted_iota(jnp.int32, (NZ, 128), 0).astype(F32)
         for i, item in enumerate(weights(rows, centre[2], offset[2])):
             high, low = split(item)
-            wz[blk, 0:128, i * 128 : i * 128 + 128] = high
-            wz[blk, 128:256, i * 128 : i * 128 + 128] = high
-            wz[blk, 256:384, i * 128 : i * 128 + 128] = low
+            wz[blk // 2, 0:128, at(i)] = high
+            wz[blk // 2, 128:256, at(i)] = high
+            wz[blk // 2, 256:384, at(i)] = low
         rows = lax.broadcasted_iota(jnp.int32, (CY, 128), 0).astype(F32)
         for i, item in enumerate(weights(rows, centre[1], offset[1])):
             wy[blk, i] = item
@@ -276,8 +286,6 @@
         centre = [item[0:1] + shift[0], item[1:2] + shift[1], item[2:3]]
         prepare(BLOCKS + f, centre, [item[3:4], item[4:5], item[5:6]], item[6:7])
 
-    own_k.wait()
-    own_u.wait()
 
     each(exists, arrived(0))
     each(exists, arrived(1))
@@ -338,8 +346,8 @@
 
         return step
 
-    lax.fori_loop(1, XU - 1, sweep(w1, wa), 0, unroll=2)
-    lax.fori_loop(2, XU - 2, sweep(wa, wb), 0, unroll=2)
+    lax.fori_loop(1, XU - 1, sweep(w1, wa), 0, unroll=10)
+    lax.fori_loop(2, XU - 2, sweep(wa, wb), 0, unroll=9)
 
     def store_split(ref, index, value):
         high, low = split(value)
@@ -353,7 +361,10 @@
             out_ref[c, x - HU] = jnp.concatenate(values[c], axis=0)[4 : 4 + CY]
         return carry
 
-    lax.fori_loop(HU, HU + CX, last, 0, unroll=2)
+    lax.fori_loop(HU, HU + CX, last, 0, unroll=8)
+
+    own_out = pltpu.make_async_copy(out_ref, out, own_sem.at[4])
+    own_out.start()
 
     def split_own(x, carry):
         for c in range(3):
@@ -362,15 +373,15 @@
             store_split(fe, (c, x, slice(None)), jnp.concatenate([field[:8], field[CY - 8 :]], axis=0))
         return carry
 
-    lax.fori_loop(0, CX, split_own, 0, unroll=2)
-
-    def contract(blk, product, row, xs, tiles, step):
+    lax.fori_loop(0, CX, split_own, 0, unroll=4)
+
+    def contract(blk, product, row, xs, tiles, step, lead):
         sums = [jnp.zeros((8, 128), F32) for _ in range(4)]
         for n, x in enumerate(xs):
             along0 = along1 = slope = bend = None
             for at, t in tiles:
                 r = row + (n * step + at) * 8
-                t0, t1, t2 = [product[r : r + 8, i * 128 : i * 128 + 128] for i in range(3)]
+                t0, t1, t2 = [product[r : r + 8, lead + i * 128 : lead + i * 128 + 128] for i in range(3)]
                 g0, g1, g2 = [wy[blk, i, t * 8 : t * 8 + 8] for i in range(3)]
                 terms = t0 * g0, t1 * g0, t0 * g1, t0 * g2 + t2 * g0
                 if along0 is None:
@@ -396,10 +407,14 @@
         else:
             xs, tiles, step = (*range(4), *range(12, 16)), ((0, 0), (1, 3)), 2
             field = jnp.concatenate([fe[c, x : x + 4].reshape(64, KZ) for c in range(3) for x in (0, 12)], axis=0)
-        product = jnp.dot(field, wz[blk], preferred_element_type=F32)
+        lead = f % 2 * 384
+        if f == 6:
+            product = jnp.dot(field, wz[blk // 2, :, 0:384], preferred_element_type=F32)
+        elif f % 2 == 0:
+            product = jnp.dot(field, wz[blk // 2], preferred_element_type=F32)
         rows = []
         for c in range(3):
-            rows += contract(blk, product, c * len(xs) * step * 8, xs, tiles, step)
+            rows += contract(blk, product, c * len(xs) * step * 8, xs, tiles, step, lead)
         part[f] = jnp.concatenate(rows + [jnp.zeros((4, 128), F32)], axis=0)
 
     def send_back(i, d):
@@ -408,16 +423,18 @@
     each(cross, send_back)
     each(same, send_back)
 
-    def own_moments(blk, carry):
-        rows = []
+    def own_moments(pair, carry):
+        rows = [[], []]
         for c in range(3):
-            product = jnp.dot(fm[c].reshape(CX * CY, KZ), wz[blk], preferred_element_type=F32)
-            rows += contract(blk, product, 0, range(CX), own_tiles, CY // 8)
-        lanes = pl.ds(pl.multiple_of(blk * 128, 128), 128)
-        total[:, lanes] = jnp.concatenate(rows + [jnp.zeros((4, 128), F32)], axis=0)
+            product = jnp.dot(fm[c].reshape(CX * CY, KZ), wz[pair], preferred_element_type=F32)
+            for i in range(2):
+                rows[i] += contract(pair * 2 + i, product, 0, range(CX), own_tiles, CY // 8, i * 384)
+        for i in range(2):
+            lanes = pl.ds(pl.multiple_of(pair * 256 + i * 128, 128), 128)
+            total[:, lanes] = jnp.concatenate(rows[i] + [jnp.zeros((4, 128), F32)], axis=0)
         return carry
 
-    lax.fori_loop(0, BLOCKS, own_moments, 0)
+    lax.fori_loop(0, BLOCKS // 2, own_moments, 0)
 
     each(exists, arrived(3))
     high, low = [], []
@@ -428,7 +445,10 @@
         low.append(rest)
     both = jnp.concatenate([jnp.concatenate(high, axis=1), jnp.concatenate(low, axis=1)], axis=0)
     spread = jnp.dot(both, gm[...], preferred_element_type=F32)
-    grad_ref[0, 0] = (total[...] + (spread[:16] + spread[16:]))[:12]
+    sums = total[...] + (spread[:16] + spread[16:])
+    for blk in range(BLOCKS):
+        grad_ref[pl.ds(blk, 12, stride=BLOCKS)] = sums[:12, blk * 128 : blk * 128 + 128]
+    own_out.wait()
 
     def sent(i, d):
         for k in range(4):
@@ -440,15 +460,15 @@
 def body(adjoint_velocity, coefficient, record_counts, record_cells, record_offsets):
     nw, nn = lax.axis_size("wide"), lax.axis_size("narrow")
     vmem = pl.BlockSpec(memory_space=pltpu.VMEM)
-    hbm = pl.BlockSpec(memory_space=pltpu.HBM)
-    return pl.pallas_call(
+    hbm = pl.BlockSpec(memory_space=pl.ANY)
+    smoothed, grads = pl.pallas_call(
         functools.partial(kernel, nw, nn),
         out_shape=(
             jax.ShapeDtypeStruct((3, CX, CY, NZ), F32),
-            jax.ShapeDtypeStruct((1, 1, 12, SLOTS), F32),
+            jax.ShapeDtypeStruct((12 * BLOCKS, 128), F32),
         ),
-        in_specs=[hbm, hbm, pl.BlockSpec(memory_space=pltpu.SMEM), vmem, vmem],
-        out_specs=(vmem, vmem),
+        in_specs=[hbm, hbm, pl.BlockSpec(memory_space=pltpu.SMEM), hbm, hbm],
+        out_specs=(hbm, vmem),
         scratch_shapes=[
             pltpu.VMEM((3, XU, YB, NZ), F32),
             pltpu.VMEM((XC, YB, NZ), F32),
@@ -458,7 +478,7 @@
             pltpu.VMEM((6, XU, YN, NZ), F32),
             pltpu.VMEM((3, CX, CY, KZ), BF16),
             pltpu.VMEM((3, CX, 16, KZ), BF16),
-            pltpu.VMEM((BLOCKS + FOREIGN, KZ, 384), BF16),
+            pltpu.VMEM(((BLOCKS + FOREIGN + 1) // 2, KZ, 768), BF16),
             pltpu.VMEM((BLOCKS + FOREIGN, 3, CY, 128), F32),
             pltpu.VMEM((BLOCKS + FOREIGN, 3, CX, 128), F32),
             pltpu.VMEM((PACKED, SLOTS), BF16),
@@ -468,12 +488,15 @@
             pltpu.VMEM((FOREIGN, 16, 128), F32),
             pltpu.VMEM((FOREIGN + 3, 16, 128), F32),
             pltpu.VMEM((16, SLOTS), F32),
-            pltpu.SemaphoreType.DMA((2,)),
+            pltpu.VMEM((3 * BLOCKS, 128), jnp.int32),
+            pltpu.VMEM((3 * BLOCKS, 128), F32),
+            pltpu.VMEM((3, CX, CY, NZ), F32),
+            pltpu.SemaphoreType.DMA((5,)),
             pltpu.SemaphoreType.DMA((4, 8)),
             pltpu.SemaphoreType.DMA((4, 8)),
         ],
         compiler_params=pltpu.CompilerParams(
-            collective_id=0, has_side_effects=True, vmem_limit_bytes=40 << 20
+            collective_id=0, has_side_effects=True, vmem_limit_bytes=63 << 20
         ),
     )(
         adjoint_velocity,
@@ -482,6 +505,7 @@
         record_cells.reshape(3 * BLOCKS, 128),
         record_offsets.reshape(3 * BLOCKS, 128),
     )
+    return smoothed, grads.reshape(1, 1, 12, SLOTS)
 
 
 def solution(mesh):

time: 44.7 us -> 40.6 us (0.908)
  the two profiles are of different devices: /device:TPU:123 before, /device:TPU:65 now
where the time goes in v3:
time: 40.6 us; the launch traced here: 40.4 us
  Pallas kernels  36.4 us (90%)
  local copies, waits for them, and re-layouts  2.7 us (7%)
  between operations  1.29 us (3%)
    pallas_call x1, Pallas kernels, body(): pl.pallas_call(functools.partial(kernel, nw, nn), out_shape=(jax.ShapeDty...  36.4 us
    unnamed x4, local copies, waits for them, and re-layouts  2.7 us

profile of v3, /device:TPU:65, one launch (start us, length us, event | category | flops | bytes accessed | tf_op | source)
XLA Modules:
  0.0 40.4 jit_solution(10647630386937237751)
XLA Ops:
  1.3 36.4 %shard_map.68 = (f32[3,16,32,128]{3,2,1,0:T(8,128)}, f32[96,128]{1,0:T(8,128)}) custom-call(f32[3,16,32,128]{3,2,1,0:T(8,128)} %u_ref.1, f32[16,32,128]{2,1,0:T(8,128)} %k_ref.1, s32[1,1]{1,0:T(1,128)S(6)} %copy.11.count_ref, s32[24,128]{1,0:T(8,128)} %bitcast.4, f32[24,128]{1,0:T(8,128)} %bitcast.5), custom_call_target="tpu_custom_call" | custom-call | tf_op jit(solution)/shard_map/pallas_call | solution.py:464
  37.7 0.0 copy-start
  37.7 2.1 %copy.12 = f32[3,16,32,128]{3,2,1,0:T(8,128)} copy(f32[3,16,32,128]{3,2,1,0:T(8,128)} %get-tuple-element.12) | data formatting | bytes 1572864
  39.8 0.0 copy-done
  39.8 0.6 %copy.13 = f32[1,1,12,1024]{3,1,2,0:T(1,128)} copy(f32[1,1,12,1024]{3,1,2,0:T(1,128)S(1)} %bitcast.3) | data formatting | bytes 98304
Async XLA Ops:
  37.7 2.1 %copy-start = (f32[96,128]{1,0:T(8,128)S(1)}, f32[96,128]{1,0:T(8,128)}, u32[]{:S(2)}) copy-start(f32[96,128]{1,0:T(8,128)} %get-tuple-element.5) | copy-start | bytes 147460

commit v4 on v3

--- a/solution.py
+++ b/solution.py
@@ -76,8 +76,8 @@
 
 
 def kernel(
-    nw, nn, u_ref, k_ref, count_ref, cells, offsets, out, grad_ref,
-    ub, cb, w1, wa, wb, ck, fm, fe, wz, wy, wx, gm, dm, mine, theirs, part, back, total, cell_ref, off_ref, out_ref,
+    nw, nn, u_ref, k_ref, counts, cells, offsets, out, grad_ref,
+    ub, cb, w1, wa, wb, ck, fm, fe, wz, wy, wx, gm, dm, mine, theirs, part, back, total, count_ref, cell_ref, off_ref, out_ref,
     own_sem, send_sem, recv_sem,
 ):
     a, b = lax.axis_index("wide"), lax.axis_index("narrow")
@@ -151,7 +151,8 @@
     own_u = pltpu.make_async_copy(u_ref, ub.at[:, pl.ds(HU, CX), pl.ds(Y0, CY)], own_sem.at[1])
     own_cells = pltpu.make_async_copy(cells, cell_ref, own_sem.at[2])
     own_offsets = pltpu.make_async_copy(offsets, off_ref, own_sem.at[3])
-    for copy in (own_cells, own_offsets, own_k, own_u):
+    own_count = pltpu.make_async_copy(counts, count_ref, own_sem.at[5])
+    for copy in (own_count, own_cells, own_offsets, own_k, own_u):
         copy.start()
 
     @pl.when(a == 0)
@@ -190,7 +191,7 @@
     def record(blk):
         centre = [cell_ref[pl.ds(d * BLOCKS + blk, 1)].astype(F32) for d in range(3)]
         offset = [off_ref[pl.ds(d * BLOCKS + blk, 1)] for d in range(3)]
-        live = jnp.where(lane1 + blk * 128 < count_ref[0, 0], 1.0, 0.0)
+        live = jnp.where(lane1 + blk * 128 < count_ref[...], 1.0, 0.0)
         return centre, offset, live
 
     def pack(blk, seen):
@@ -223,6 +224,7 @@
         dm[:, lanes] = jnp.concatenate(pieces, axis=0).astype(BF16)
         return seen + jnp.sum(member, axis=1, keepdims=True)
 
+    own_count.wait()
     own_cells.wait()
     own_offsets.wait()
     lax.fori_loop(0, BLOCKS, pack, jnp.zeros((8, 128), F32))
@@ -320,7 +322,7 @@
                 w1[c, x, r : r + 8] = scale * ub[c, x, r : r + 8]
         return carry
 
-    lax.fori_loop(0, XU, face_coefficients, 0, unroll=2)
+    lax.fori_loop(0, XU, face_coefficients, 0, unroll=11)
 
     def relaxed(src, x):
         values = [[], [], []]
@@ -373,7 +375,7 @@
             store_split(fe, (c, x, slice(None)), jnp.concatenate([field[:8], field[CY - 8 :]], axis=0))
         return carry
 
-    lax.fori_loop(0, CX, split_own, 0, unroll=4)
+    lax.fori_loop(0, CX, split_own, 0, unroll=8)
 
     def contract(blk, product, row, xs, tiles, step, lead):
         sums = [jnp.zeros((8, 128), F32) for _ in range(4)]
@@ -434,7 +436,7 @@
             total[:, lanes] = jnp.concatenate(rows[i] + [jnp.zeros((4, 128), F32)], axis=0)
         return carry
 
-    lax.fori_loop(0, BLOCKS // 2, own_moments, 0)
+    lax.fori_loop(0, BLOCKS // 2, own_moments, 0, unroll=2)
 
     each(exists, arrived(3))
     high, low = [], []
@@ -467,7 +469,7 @@
             jax.ShapeDtypeStruct((3, CX, CY, NZ), F32),
             jax.ShapeDtypeStruct((12 * BLOCKS, 128), F32),
         ),
-        in_specs=[hbm, hbm, pl.BlockSpec(memory_space=pltpu.SMEM), hbm, hbm],
+        in_specs=[hbm, hbm, hbm, hbm, hbm],
         out_specs=(hbm, vmem),
         scratch_shapes=[
             pltpu.VMEM((3, XU, YB, NZ), F32),
@@ -488,10 +490,11 @@
             pltpu.VMEM((FOREIGN, 16, 128), F32),
             pltpu.VMEM((FOREIGN + 3, 16, 128), F32),
             pltpu.VMEM((16, SLOTS), F32),
+            pltpu.VMEM((1, 1), jnp.int32),
             pltpu.VMEM((3 * BLOCKS, 128), jnp.int32),
             pltpu.VMEM((3 * BLOCKS, 128), F32),
             pltpu.VMEM((3, CX, CY, NZ), F32),
-            pltpu.SemaphoreType.DMA((5,)),
+            pltpu.SemaphoreType.DMA((6,)),
             pltpu.SemaphoreType.DMA((4, 8)),
             pltpu.SemaphoreType.DMA((4, 8)),
         ],

time: 40.6 us -> 39.9 us (0.983)
  Pallas kernels: 36.4 us -> 35.8 us
    pallas_call x1, Pallas kernels: 36.4 us -> 35.8 us  [body(): pl.pallas_call(functools.partial(kernel, nw, nn), out_shape=(jax.ShapeDty...]
where the time goes in v4:
time: 39.9 us; the launch traced here: 39.7 us
  Pallas kernels  35.8 us (90%)
  local copies, waits for them, and re-layouts  2.7 us (7%)
  between operations  1.29 us (3%)
    pallas_call x1, Pallas kernels, body(): pl.pallas_call(functools.partial(kernel, nw, nn), out_shape=(jax.ShapeDty...  35.8 us
    unnamed x4, local copies, waits for them, and re-layouts  2.7 us

profile of v4, /device:TPU:65, one launch (start us, length us, event | category | flops | bytes accessed | tf_op | source)
XLA Modules:
  0.0 39.7 jit_solution(641830966806333285)
XLA Ops:
  1.3 35.8 %shard_map.68 = (f32[3,16,32,128]{3,2,1,0:T(8,128)}, f32[96,128]{1,0:T(8,128)}) custom-call(f32[3,16,32,128]{3,2,1,0:T(8,128)} %u_ref.1, f32[16,32,128]{2,1,0:T(8,128)} %k_ref.1, s32[1,1]{1,0:T(1,128)S(6)} %copy.11.counts, s32[24,128]{1,0:T(8,128)} %bitcast.4, f32[24,128]{1,0:T(8,128)} %bitcast.5), custom_call_target="tpu_custom_call" | custom-call | tf_op jit(solution)/shard_map/pallas_call | solution.py:466
  37.0 0.0 copy-start
  37.0 2.1 %copy.12 = f32[3,16,32,128]{3,2,1,0:T(8,128)} copy(f32[3,16,32,128]{3,2,1,0:T(8,128)} %get-tuple-element.12) | data formatting | bytes 1572864
  39.1 0.0 copy-done
  39.1 0.6 %copy.13 = f32[1,1,12,1024]{3,1,2,0:T(1,128)} copy(f32[1,1,12,1024]{3,1,2,0:T(1,128)S(1)} %bitcast.3) | data formatting | bytes 98304
Async XLA Ops:
  37.0 2.1 %copy-start = (f32[96,128]{1,0:T(8,128)S(1)}, f32[96,128]{1,0:T(8,128)}, u32[]{:S(2)}) copy-start(f32[96,128]{1,0:T(8,128)} %get-tuple-element.5) | copy-start | bytes 147460

commit v5 on v4

--- a/solution.py
+++ b/solution.py
@@ -398,7 +398,11 @@
         return [jnp.sum(item, axis=0, keepdims=True) for item in sums]
 
     own_tiles = tuple((t, t) for t in range(CY // 8))
-    for f in range(FOREIGN):
+    def send_back(turned, i, d):
+        if bool(d[1]) == turned:
+            copy_of(3, i, d).start()
+
+    for f in (4, 5, 6, 0, 1, 2, 3):
         blk = BLOCKS + f
         if f < 4:
             xs, tiles, step = range(12, 16) if f < 2 else range(4), own_tiles, CY // 8
@@ -418,12 +422,11 @@
         for c in range(3):
             rows += contract(blk, product, c * len(xs) * step * 8, xs, tiles, step, lead)
         part[f] = jnp.concatenate(rows + [jnp.zeros((4, 128), F32)], axis=0)
-
-    def send_back(i, d):
-        copy_of(3, i, d).start()
-
-    each(cross, send_back)
-    each(same, send_back)
+        if f == 6:
+            each(cross, functools.partial(send_back, True))
+            each(same, functools.partial(send_back, True))
+    each(same, functools.partial(send_back, False))
+
 
     def own_moments(pair, carry):
         rows = [[], []]

time: 39.9 us -> 39.3 us (0.985)
  Pallas kernels: 35.8 us -> 35.1 us
    pallas_call x1, Pallas kernels: 35.8 us -> 35.1 us  [body(): pl.pallas_call(functools.partial(kernel, nw, nn), out_shape=(jax.ShapeDty...]
where the time goes in v5:
time: 39.3 us; the launch traced here: 39.1 us
  Pallas kernels  35.1 us (89%)
  local copies, waits for them, and re-layouts  2.7 us (7%)
  between operations  1.29 us (3%)
    pallas_call x1, Pallas kernels, body(): pl.pallas_call(functools.partial(kernel, nw, nn), out_shape=(jax.ShapeDty...  35.1 us
    unnamed x4, local copies, waits for them, and re-layouts  2.7 us

profile of v5, /device:TPU:65, one launch (start us, length us, event | category | flops | bytes accessed | tf_op | source)
XLA Modules:
  0.0 39.1 jit_solution(16835025598812268371)
XLA Ops:
  1.3 35.1 %shard_map.68 = (f32[3,16,32,128]{3,2,1,0:T(8,128)}, f32[96,128]{1,0:T(8,128)}) custom-call(f32[3,16,32,128]{3,2,1,0:T(8,128)} %u_ref.1, f32[16,32,128]{2,1,0:T(8,128)} %k_ref.1, s32[1,1]{1,0:T(1,128)S(6)} %copy.11.counts, s32[24,128]{1,0:T(8,128)} %bitcast.4, f32[24,128]{1,0:T(8,128)} %bitcast.5), custom_call_target="tpu_custom_call" | custom-call | tf_op jit(solution)/shard_map/pallas_call | solution.py:469
  36.4 0.0 copy-start
  36.4 2.1 %copy.12 = f32[3,16,32,128]{3,2,1,0:T(8,128)} copy(f32[3,16,32,128]{3,2,1,0:T(8,128)} %get-tuple-element.12) | data formatting | bytes 1572864
  38.5 0.0 copy-done
  38.5 0.6 %copy.13 = f32[1,1,12,1024]{3,1,2,0:T(1,128)} copy(f32[1,1,12,1024]{3,1,2,0:T(1,128)S(1)} %bitcast.3) | data formatting | bytes 98304
Async XLA Ops:
  36.4 2.1 %copy-start = (f32[96,128]{1,0:T(8,128)S(1)}, f32[96,128]{1,0:T(8,128)}, u32[]{:S(2)}) copy-start(f32[96,128]{1,0:T(8,128)} %get-tuple-element.5) | copy-start | bytes 147460
